TPU v7x, 1024 devices: a whole 8x8x8 slice. The times are simulated.
1024 devices in a mesh: lat: 16 (over y, core), lon: 64 (over x, z).
Axes of the slice: x: 8, y: 8, z: 8, core: 2. Of those that a mesh axis runs over, the one named last changes fastest.
Arguments:
- layer_temp: float32 [256, 35, 8192], P('lat', None, 'lon'), may hold values from -20 to -2
- ice_depth_per_class: float32 [256, 5, 8192], P('lat', None, 'lon'), may hold values from 0.5 to 3
- ice_area: float32 [256, 5, 8192], P('lat', None, 'lon'), may hold values from 0.05 to 0.2
- surf_temp: float32 [256, 8192], P('lat', 'lon'), may hold values from -30 to -2
- seawater_thermal_input: float32 [256, 8192], P('lat', 'lon'), may hold values from 0 to 0.3
- velocity: float32 [2, 256, 8192], P(None, 'lat', 'lon'), may hold values from -1.2 to 1.2
- stress: float32 [3, 256, 8192], P(None, 'lat', 'lon'), may hold values from -3 to 3
- wind_stress: float32 [2, 256, 8192], P(None, 'lat', 'lon'), may hold values from -1.8 to 1.8
- current: float32 [2, 256, 8192], P(None, 'lat', 'lon'), may hold values from -1.8 to 1.8
- land_mask: int32 [256, 8192], P('lat', 'lon'), may hold values 0 or 1
- ice_mask: int32 [64, 256], P('lon', 'lat'), may hold values from 0 to 1, as said below
- band_index: int32 [256], P('lat'), may hold values from 0 to 63, as said below
Outputs:
- temp_after: float32 [256, 35, 8192], P('lat', None, 'lon')
- thick_after: float32 [256, 5, 8192], P('lat', None, 'lon')
- velocity_after: float32 [2, 256, 8192], P(None, 'lat', 'lon')
- stress_after: float32 [3, 256, 8192], P(None, 'lat', 'lon')
- zonal_volume: float32 [64], P('lat')
Inputs may be any that keep to these rules, and one draw needn't show every extreme that they name: `ice_mask`: for each lat index, the strips of all devices with that index include at most 448 ice-covered strips and more than (6) times the number of lon devices; among these devices one has all its 16 strips ice-covered. `band_index`: every band holds 1 to 7 rows, which lie next to one another; one band holds exactly 7.
All inputs are finite; a program needn't handle non-finite values. No bound on the sum of `land_mask` on one device may be relied on, other than what follows from the above.
Results may differ from a plain program's by a relative error of at most 0.00002.
Values sent between devices are 32-bit elements; how exact they have to be, the bound alone decides.
No kernel may reach another device: no remote copies, remote signals or barrier semaphores. Data moves between devices by JAX's collectives and lax.ppermute only.
A program may use at most 32 MiB of HBM per device.

v0:
```python
import jax
import jax.numpy as jnp
from jax import lax
from jax.sharding import PartitionSpec as P

DEPTH_CLASSES = 5
VERTICAL_LEVELS = 7
SUBCYCLES = 3
SWEEPS = 2
BANDS_DEV = 4


FREEZE_POINT = -1.8
BASE_CONDUCT = 2.03
SALT_CONDUCT = 0.416
CONDUCT_SCALE = 1.0
GROWTH_RATE = 0.02
STRENGTH_SCALE = 1.0
STRENGTH_DECAY = 5.0
ELLIPSE_SQUARE = 4.0
STRAIN_FLOOR = 0.0025
STRESS_RELAX = 0.5
MOMENTUM_STEP = 0.5
WATER_DRAG = 1.0


def with_halo(value, sides, width):
    for axis, dim in sides:
        size, length = (lax.axis_size(axis), value.shape[dim])
        up = [(i, (i + 1) % size) for i in range(size)]
        down = [(j, i) for i, j in up]
        last = lax.slice_in_dim(value, length - width, length, axis=dim)
        leading = lax.slice_in_dim(value, 0, width, axis=dim)
        before = lax.ppermute(last, axis, up)
        after = lax.ppermute(leading, axis, down)
        value = jnp.concatenate([before, value, after], axis=dim)
    return value


def split_up(value, dim, length):
    before, after = (value.shape[:dim], value.shape[dim + 1 :])
    return jnp.moveaxis(value.reshape(*before, length, -1, *after), dim, 0)


def sent_and_summed(value, axis, dim):
    pieces = split_up(value, dim, lax.axis_size(axis))
    arrived = lax.all_to_all(pieces, axis, split_axis=0, concat_axis=0, tiled=True)
    return arrived.sum(axis=0)


def sent_to_all(value, axis):
    length = lax.axis_size(axis)
    return lax.all_to_all(
        jnp.broadcast_to(value[None], (length, *value.shape)), axis, 0, 0, tiled=True
    )


def over_copies(value, axis):
    return sent_to_all(value, axis).sum(axis=0)


def together(arrays, axis):
    flat, at, gathered = (jnp.concatenate([a.reshape(-1) for a in arrays]), 0, [])
    subtotal = over_copies(flat, axis)
    for a in arrays:
        gathered.append(subtotal[at : at + a.size].reshape(a.shape))
        at += a.size
    return tuple(gathered)


def update_vertical_cell(
    thermal_state_levels, ice_depth_per_class, upper_interface_state, seawater_thermal_input
):
    first_extent = thermal_state_levels.shape[:-2]
    vertical_cell_group = thermal_state_levels.shape[-1]
    vertical_levels_state = thermal_state_levels.reshape(
        first_extent + (DEPTH_CLASSES, VERTICAL_LEVELS, vertical_cell_group)
    )
    before = [vertical_levels_state[..., layer_at, :] for layer_at in range(VERTICAL_LEVELS)]
    surface_row = upper_interface_state[..., None, :]
    scaled = CONDUCT_SCALE / (ice_depth_per_class * ice_depth_per_class)
    repeated_pass = before
    for picard_turn in range(SWEEPS):
        conductance = [BASE_CONDUCT + SALT_CONDUCT / guessed for guessed in repeated_pass]
        couplings = [scaled * conductance[0]]
        for layer_at in range(1, VERTICAL_LEVELS):
            couplings.append(scaled * 0.5 * (conductance[layer_at - 1] + conductance[layer_at]))
        couplings.append(scaled * conductance[VERTICAL_LEVELS - 1])
        upper_ratio = []
        eliminated = []
        for layer_at in range(VERTICAL_LEVELS):
            source_term = before[layer_at]
            divisor = 1.0 + couplings[layer_at] + couplings[layer_at + 1]
            if layer_at == 0:
                source_term = source_term + couplings[0] * surface_row
            else:
                divisor = divisor - couplings[layer_at] * upper_ratio[layer_at - 1]
                source_term = source_term + couplings[layer_at] * eliminated[layer_at - 1]
            if layer_at == VERTICAL_LEVELS - 1:
                source_term = source_term + couplings[VERTICAL_LEVELS] * FREEZE_POINT
            upper_ratio.append(couplings[layer_at + 1] / divisor)
            eliminated.append(source_term / divisor)
        solved = list(eliminated)
        for layer_at in range(VERTICAL_LEVELS - 2, -1, -1):
            solved[layer_at] = eliminated[layer_at] + upper_ratio[layer_at] * solved[layer_at + 1]
        repeated_pass = solved
    bottom = repeated_pass[VERTICAL_LEVELS - 1]
    regrown = (
        ice_depth_per_class
        + GROWTH_RATE
        * (BASE_CONDUCT + SALT_CONDUCT / bottom)
        * (FREEZE_POINT - bottom)
        / ice_depth_per_class
        - seawater_thermal_input[..., None, :]
    )
    updated_vertical_cells = jnp.stack(repeated_pass, axis=-2).reshape(thermal_state_levels.shape)
    return (updated_vertical_cells, regrown)


def stress_update(zonal_field, meridional_field, previous, strength):
    zonal_east = (zonal_field[1:-1, 2:] - zonal_field[1:-1, :-2]) * 0.5
    zonal_north = (zonal_field[2:, 1:-1] - zonal_field[:-2, 1:-1]) * 0.5
    meridional_east = (meridional_field[1:-1, 2:] - meridional_field[1:-1, :-2]) * 0.5
    meridional_north = (meridional_field[2:, 1:-1] - meridional_field[:-2, 1:-1]) * 0.5
    divergence = zonal_east + meridional_north
    tension = zonal_east - meridional_north
    shearing = zonal_north + meridional_east
    deformation = jnp.sqrt(
        divergence * divergence
        + (tension * tension + shearing * shearing) / ELLIPSE_SQUARE
        + STRAIN_FLOOR
    )
    viscous = strength / deformation
    bulk_new = (previous[0] + STRESS_RELAX * viscous * (divergence - deformation)) / (
        1.0 + STRESS_RELAX
    )
    tension_new = (previous[1] + STRESS_RELAX * viscous * tension / ELLIPSE_SQUARE) / (
        1.0 + STRESS_RELAX
    )
    shear_new = (previous[2] + STRESS_RELAX * viscous * shearing / (2.0 * ELLIPSE_SQUARE)) / (
        1.0 + STRESS_RELAX
    )
    return jnp.stack([bulk_new, tension_new, shear_new])


def force_update(padded, velocity, ice_mass, wind_stress, current, wet_cells):
    normal_east = 0.5 * (padded[0] + padded[1])
    normal_north = 0.5 * (padded[0] - padded[1])
    shear_stress = padded[2]
    push_east = (normal_east[1:-1, 2:] - normal_east[1:-1, :-2]) * 0.5 + (
        shear_stress[2:, 1:-1] - shear_stress[:-2, 1:-1]
    ) * 0.5
    push_north = (shear_stress[1:-1, 2:] - shear_stress[1:-1, :-2]) * 0.5 + (
        normal_north[2:, 1:-1] - normal_north[:-2, 1:-1]
    ) * 0.5
    pushes = jnp.stack([push_east, push_north])
    moved = velocity + MOMENTUM_STEP * (pushes / ice_mass + wind_stress + WATER_DRAG * current)
    return wet_cells * moved / (1.0 + MOMENTUM_STEP * WATER_DRAG)


def local(
    layer_temp,
    ice_depth_per_class,
    ice_area,
    surf_temp,
    seawater_thermal_input,
    velocity,
    stress,
    wind_stress,
    current,
    land_mask,
    ice_mask,
    band_index,
):
    rows_here = layer_temp.shape[0]
    cols_here = layer_temp.shape[2]
    lat_here = lax.axis_index("lat")
    lat_size = lax.axis_size("lat")
    volume_start = jnp.sum(ice_area * ice_depth_per_class, axis=1)
    coverage = jnp.sum(ice_area, axis=1)
    strength = STRENGTH_SCALE * volume_start * jnp.exp(-STRENGTH_DECAY * (1.0 - coverage))
    ice_mass = 1.0 + volume_start
    wet_cells = land_mask.astype(jnp.float32)
    row_ids = jnp.arange(rows_here + 4)
    outside = (lat_here == 0) & (row_ids < 2) | (lat_here == lat_size - 1) & (
        row_ids >= rows_here + 2
    )
    moving = velocity
    stresses = stress
    for subcycle in range(SUBCYCLES):
        stacked = jnp.concatenate([moving, stresses, strength[None]], axis=0)
        widened = with_halo(stacked, (("lat", 1), ("lon", 2)), 2)
        widened = jnp.where(outside[None, :, None], 0.0, widened)
        margin_stress = stress_update(
            widened[0], widened[1], widened[2:5, 1:-1, 1:-1], widened[5, 1:-1, 1:-1]
        )
        moving = force_update(margin_stress, moving, ice_mass, wind_stress, current, wet_cells)
        stresses = margin_stress[:, 1:-1, 1:-1]
    ice_rows = ice_mask[0]
    stepped_temp, stepped_thick = update_vertical_cell(
        layer_temp, ice_depth_per_class, surf_temp, seawater_thermal_input
    )
    strip_ice = (ice_rows == 1)[:, None, None]
    temp_after = jnp.where(strip_ice, stepped_temp, layer_temp)
    thick_after = jnp.where(strip_ice, stepped_thick, ice_depth_per_class)
    volume_after = jnp.sum(ice_area * thick_after, axis=1)
    row_total = jnp.sum(volume_after, axis=1)
    band_count = BANDS_DEV * lat_size
    members = (band_index[:, None] == jnp.arange(band_count, dtype=jnp.int32)[None, :]).astype(
        jnp.float32
    )
    part_sum = jnp.sum(members * row_total[:, None], axis=0)
    part_cells = jnp.sum(members, axis=0) * cols_here
    row_sum, row_cells = (
        sent_and_summed(part_sum, "lat", 0),
        sent_and_summed(part_cells, "lat", 0),
    )
    share_sum, share_cells = together((row_sum, row_cells), "lon")
    zonal_volume = share_sum / share_cells
    return (temp_after, thick_after, moving, stresses, zonal_volume)


def solution(mesh):
    return jax.shard_map(
        local,
        mesh=mesh,
        in_specs=(
            P("lat", None, "lon"),
            P("lat", None, "lon"),
            P("lat", None, "lon"),
            P("lat", "lon"),
            P("lat", "lon"),
            P(None, "lat", "lon"),
            P(None, "lat", "lon"),
            P(None, "lat", "lon"),
            P(None, "lat", "lon"),
            P("lat", "lon"),
            P("lon", "lat"),
            P("lat"),
        ),
        out_specs=(
            P("lat", None, "lon"),
            P("lat", None, "lon"),
            P(None, "lat", "lon"),
            P(None, "lat", "lon"),
            P("lat"),
        ),
        check_vma=False,
    )
```

profile of v0, /device:TPU:1, one launch (start us, length us, event | category | flops | bytes accessed | tf_op | source)
XLA Modules:
  0.0 97.3 jit_solution(2685284979461985533)
XLA Ops:
  1.3 1.1 %add_divide_fusion.6 = (f32[16,5,128]{2,0,1:T(8,128)S(1)}, f32[16,5,128]{2,0,1:T(8,128)S(1)}, f32[16,5,128]{2,0,1:T(8,128)S(1)}, f32[16,5,128]{2,0,1:T(8,128)S(1...) fusion(f32[16,5,7,128]{3,0,2,1:T(8,128)} %bitcast.330, ...), kind=kLoop, calls=%fused_computation.92 | loop fusion | flops 768000 | bytes 786432 | tf_op jit(solution)/shard_map/div | solution.py:102
  3.3 1.0 %multiply_reduce_fusion = (f32[16]{0:T(128)S(1)}, f32[16,128]{1,0:T(8,128)S(1)}, f32[16,128]{1,0:T(8,128)S(1)}, f32[16,5,128]{2,0,1:T(8,128)}, f32[16,5,128]{2,0...) fusion(f32[16,5,128]{2,0,1:T(8,128)S(1)} %copy-done.7, ...), kind=kLoop, calls=%fused_computation.48 | loop fusion | flops 1316848 | bytes 1261648 | tf_op jit(solution)/shard_map/reduce_sum | solution.py:207
  4.3 0.7 copy-done.2
  5.0 14.2 %collective-permute-start.1 = (f32[6,2,128]{2,1,0:T(2,128)S(1)}, f32[6,2,128]{2,1,0:T(2,128)S(1)}, u32[]{:S(2)}, u32[]{:S(2)}) collective-permute-start(f32[6,2,128]{2,1,0:T(2,128)S(1)} %get-tuple-element.76), channel_id=1, source_target_pairs={{64,0},{128,64},{192,128},{256,192},{320,256},{384,320},{448,384},... | collective-permute-start | bytes 18440 | tf_op jit(solution)/shard_map/ppermute | solution.py:35
  19.9 0.7 mul.551
  20.6 3.6 %all-to-all-start.1 = ((f32[16,1,4]{2,1,0:T(1,128)}), f32[16,1,4]{2,1,0:T(1,128)S(1)}, u32[]{:S(2)}, u32[]{:S(2)}) async-start(f32[16,1,4]{2,1,0:T(1,128)} %bitcast.52), calls=%async_computation.1 | async-start | bytes 16384 | tf_op jit(solution)/shard_map/all_to_all | solution.py:47
  24.6 11.2 %collective-permute-start.3 = (f32[6,20,2]{2,1,0:T(8,128)S(1)}, f32[6,20,2]{2,1,0:T(8,128)S(1)}, u32[]{:S(2)}, u32[]{:S(2)}) collective-permute-start(f32[6,20,2]{2,1,0:T(8,128)S(1)} %get-tuple-element.70), channel_id=1, source_target_pairs={{1,0},{2,1},{3,2},{4,3},{5,4},{6,5},{7,6},{8,7},{9,8},{10,9},{11,1... | collective-permute-start | bytes 2888 | tf_op jit(solution)/shard_map/ppermute | solution.py:35
  35.8 1.9 %collective-permute-start.2 = (f32[6,20,2]{2,1,0:T(8,128)S(1)}, f32[6,20,2]{2,1,0:T(8,128)S(1)}, u32[]{:S(2)}, u32[]{:S(2)}) collective-permute-start(f32[6,20,2]{2,1,0:T(8,128)S(1)} %get-tuple-element.69), channel_id=1, source_target_pairs={{0,1},{1,2},{2,3},{3,4},{4,5},{5,6},{6,7},{7,8},{8,9},{9,10},{10,1... | collective-permute-start | bytes 2888 | tf_op jit(solution)/shard_map/ppermute | solution.py:34
  37.8 0.7 all_to_all.14
  38.5 5.8 %collective-permute-done.2 = f32[6,20,2]{2,1,0:T(8,128)S(1)} collective-permute-done((f32[6,20,2]{2,1,0:T(8,128)S(1)}, f32[6,20,2]{2,1,0:T(8,128)S(1)}, u32[]{:S(2)}, u32[]{:S(2)}) %collective-permute-start.2) | collective-permute-done | bytes 992 | tf_op jit(solution)/shard_map/ppermute | solution.py:34
  45.5 1.5 %collective-permute-start.5 = (f32[6,2,128]{2,1,0:T(2,128)S(1)}, f32[6,2,128]{2,1,0:T(2,128)S(1)}, u32[]{:S(2)}, u32[]{:S(2)}) collective-permute-start(f32[6,2,128]{2,1,0:T(2,128)S(1)} %get-tuple-element.74), channel_id=1, source_target_pairs={{64,0},{128,64},{192,128},{256,192},{320,256},{384,320},{448,384},... | collective-permute-start | bytes 18440 | tf_op jit(solution)/shard_map/ppermute | solution.py:35
  47.0 1.6 %collective-permute-start.4 = (f32[6,2,128]{2,1,0:T(2,128)S(1)}, f32[6,2,128]{2,1,0:T(2,128)S(1)}, u32[]{:S(2)}, u32[]{:S(2)}) collective-permute-start(f32[6,2,128]{2,1,0:T(2,128)S(1)} %get-tuple-element.73), channel_id=1, source_target_pairs={{0,64},{64,128},{128,192},{192,256},{256,320},{320,384},{384,448},... | collective-permute-start | bytes 18440 | tf_op jit(solution)/shard_map/ppermute | solution.py:34
  48.6 6.1 %all-to-all-start = ((f32[16,1,4]{2,1,0:T(1,128)}), f32[16,1,4]{2,1,0:T(1,128)S(1)}, u32[]{:S(2)}, u32[]{:S(2)}) async-start(f32[16,1,4]{2,1,0:T(1,128)} %bitcast.51), calls=%async_computation | async-start | bytes 16384 | tf_op jit(solution)/shard_map/all_to_all | solution.py:47
  54.7 6.9 %all-to-all-done = f32[16,1,4]{2,1,0:T(1,128)S(1)} async-done(((f32[16,1,4]{2,1,0:T(1,128)}), f32[16,1,4]{2,1,0:T(1,128)S(1)}, u32[]{:S(2)}, u32[]{:S(2)}) %all-to-all-start) | async-done | bytes 288 | tf_op jit(solution)/shard_map/all_to_all | solution.py:47
  61.8 1.9 %collective-permute-start.7 = (f32[6,20,2]{2,1,0:T(8,128)S(1)}, f32[6,20,2]{2,1,0:T(8,128)S(1)}, u32[]{:S(2)}, u32[]{:S(2)}) collective-permute-start(f32[6,20,2]{2,1,0:T(8,128)S(1)} %get-tuple-element.68), channel_id=1, source_target_pairs={{1,0},{2,1},{3,2},{4,3},{5,4},{6,5},{7,6},{8,7},{9,8},{10,9},{11,1... | collective-permute-start | bytes 2888 | tf_op jit(solution)/shard_map/ppermute | solution.py:35
  63.7 3.4 %collective-permute-start.6 = (f32[6,20,2]{2,1,0:T(8,128)S(1)}, f32[6,20,2]{2,1,0:T(8,128)S(1)}, u32[]{:S(2)}, u32[]{:S(2)}) collective-permute-start(f32[6,20,2]{2,1,0:T(8,128)S(1)} %get-tuple-element.67), channel_id=1, source_target_pairs={{0,1},{1,2},{2,3},{3,4},{4,5},{5,6},{6,7},{7,8},{8,9},{9,10},{10,1... | collective-permute-start | bytes 2888 | tf_op jit(solution)/shard_map/ppermute | solution.py:34
  67.8 6.1 %all-to-all-start.2 = ((f32[64,1,8]{2,1,0:T(1,128)}), f32[64,1,8]{2,1,0:T(1,128)S(1)}, u32[]{:S(2)}, u32[]{:S(2)}) async-start(f32[64,1,8]{2,1,0:T(1,128)} %broadcast_in_dim.64), calls=%async_computation.2 | async-start | bytes 65536 | tf_op jit(solution)/shard_map/all_to_all | solution.py:53
  74.5 1.2 %collective-permute-start.9 = (f32[6,2,128]{2,1,0:T(2,128)S(1)}, f32[6,2,128]{2,1,0:T(2,128)S(1)}, u32[]{:S(2)}, u32[]{:S(2)}) collective-permute-start(f32[6,2,128]{2,1,0:T(2,128)S(1)} %get-tuple-element.72), channel_id=1, source_target_pairs={{64,0},{128,64},{192,128},{256,192},{320,256},{384,320},{448,384},... | collective-permute-start | bytes 18440 | tf_op jit(solution)/shard_map/ppermute | solution.py:35
  76.3 0.8 bitcast_select_fusion
  77.1 7.6 %all-to-all-done.2 = f32[64,1,8]{2,1,0:T(1,128)S(1)} async-done(((f32[64,1,8]{2,1,0:T(1,128)}), f32[64,1,8]{2,1,0:T(1,128)S(1)}, u32[]{:S(2)}, u32[]{:S(2)}) %all-to-all-start.2) | async-done | bytes 2080 | tf_op jit(solution)/shard_map/all_to_all | solution.py:53
  84.9 2.2 %collective-permute-start.11 = (f32[6,20,2]{2,1,0:T(8,128)S(1)}, f32[6,20,2]{2,1,0:T(8,128)S(1)}, u32[]{:S(2)}, u32[]{:S(2)}) collective-permute-start(f32[6,20,2]{2,1,0:T(8,128)S(1)} %get-tuple-element.66), channel_id=1, source_target_pairs={{1,0},{2,1},{3,2},{4,3},{5,4},{6,5},{7,6},{8,7},{9,8},{10,9},{11,1... | collective-permute-start | bytes 2888 | tf_op jit(solution)/shard_map/ppermute | solution.py:35
  87.1 3.1 %collective-permute-start.10 = (f32[6,20,2]{2,1,0:T(8,128)S(1)}, f32[6,20,2]{2,1,0:T(8,128)S(1)}, u32[]{:S(2)}, u32[]{:S(2)}) collective-permute-start(f32[6,20,2]{2,1,0:T(8,128)S(1)} %get-tuple-element.65), channel_id=1, source_target_pairs={{0,1},{1,2},{2,3},{3,4},{4,5},{5,6},{6,7},{7,8},{8,9},{9,10},{10,1... | collective-permute-start | bytes 2888 | tf_op jit(solution)/shard_map/ppermute | solution.py:34
  90.8 4.8 %collective-permute-done.10 = f32[6,20,2]{2,1,0:T(8,128)S(1)} collective-permute-done((f32[6,20,2]{2,1,0:T(8,128)S(1)}, f32[6,20,2]{2,1,0:T(8,128)S(1)}, u32[]{:S(2)}, u32[]{:S(2)}) %collective-permute-start.10) | collective-permute-done | bytes 992 | tf_op jit(solution)/shard_map/ppermute | solution.py:34
  96.6 0.7 pad_maximum_fusion.9
  (89 shorter events, 7.7 us)
Async XLA Ops:
  1.3 1.1 %copy-start = (f32[16,35,128]{2,0,1:T(8,128)S(1)}, f32[16,35,128]{2,0,1:T(8,128)}, u32[]{:S(2)}) copy-start(f32[16,35,128]{2,0,1:T(8,128)} %param.12) | copy-start | bytes 860164
  1.3 1.1 %copy-start.1 = (f32[16,5,128]{2,0,1:T(8,128)S(1)}, f32[16,5,128]{2,0,1:T(8,128)}, u32[]{:S(2)}) copy-start(f32[16,5,128]{2,0,1:T(8,128)} %param.13) | copy-start | bytes 122884
  2.4 0.8 copy-start.7
  2.5 0.8 copy-start.8
  3.3 1.0 %copy-start.3 = (f32[3,16,128]{2,1,0:T(8,128)S(1)}, f32[3,16,128]{2,1,0:T(8,128)}, u32[]{:S(2)}) copy-start(f32[3,16,128]{2,1,0:T(8,128)} %param.18) | copy-start | bytes 73732
  4.3 0.7 copy-start.2
  5.0 19.5 %collective-permute-start.1 = (f32[6,2,128]{2,1,0:T(2,128)S(1)}, f32[6,2,128]{2,1,0:T(2,128)S(1)}, u32[]{:S(2)}, u32[]{:S(2)}) collective-permute-start(f32[6,2,128]{2,1,0:T(2,128)S(1)} %get-tuple-element.76), channel_id=1, source_target_pairs={{64,0},{128,64},{192,128},{256,192},{320,256},{384,320},{448,384},... | collective-permute-start | bytes 18440 | tf_op jit(solution)/shard_map/ppermute | solution.py:35
  19.2 5.3 %collective-permute-start = (f32[6,2,128]{2,1,0:T(2,128)S(1)}, f32[6,2,128]{2,1,0:T(2,128)S(1)}, u32[]{:S(2)}, u32[]{:S(2)}) collective-permute-start(f32[6,2,128]{2,1,0:T(2,128)S(1)} %get-tuple-element.75), channel_id=1, source_target_pairs={{0,64},{64,128},{128,192},{192,256},{256,320},{320,384},{384,448},... | collective-permute-start | bytes 18440 | tf_op jit(solution)/shard_map/ppermute | solution.py:34
  20.6 28.0 %all-to-all-start.1 = ((f32[16,1,4]{2,1,0:T(1,128)}), f32[16,1,4]{2,1,0:T(1,128)S(1)}, u32[]{:S(2)}, u32[]{:S(2)}) async-start(f32[16,1,4]{2,1,0:T(1,128)} %bitcast.52), calls=%async_computation.1 | async-start | bytes 16384 | tf_op jit(solution)/shard_map/all_to_all | solution.py:47
  24.5 13.2 %copy-start.9 = (s32[16,128]{1,0:T(8,128)S(1)}, s32[16,128]{1,0:T(8,128)}, u32[]{:S(2)}) copy-start(s32[16,128]{1,0:T(8,128)} %param.21) | copy-start | bytes 24580
  24.6 13.9 %collective-permute-start.3 = (f32[6,20,2]{2,1,0:T(8,128)S(1)}, f32[6,20,2]{2,1,0:T(8,128)S(1)}, u32[]{:S(2)}, u32[]{:S(2)}) collective-permute-start(f32[6,20,2]{2,1,0:T(8,128)S(1)} %get-tuple-element.70), channel_id=1, source_target_pairs={{1,0},{2,1},{3,2},{4,3},{5,4},{6,5},{7,6},{8,7},{9,8},{10,9},{11,1... | collective-permute-start | bytes 2888 | tf_op jit(solution)/shard_map/ppermute | solution.py:35
  35.8 8.4 %collective-permute-start.2 = (f32[6,20,2]{2,1,0:T(8,128)S(1)}, f32[6,20,2]{2,1,0:T(8,128)S(1)}, u32[]{:S(2)}, u32[]{:S(2)}) collective-permute-start(f32[6,20,2]{2,1,0:T(8,128)S(1)} %get-tuple-element.69), channel_id=1, source_target_pairs={{0,1},{1,2},{2,3},{3,4},{4,5},{5,6},{6,7},{7,8},{8,9},{9,10},{10,1... | collective-permute-start | bytes 2888 | tf_op jit(solution)/shard_map/ppermute | solution.py:34
  44.7 0.7 copy-start.4
  44.7 0.7 copy-start.5
  45.5 16.1 %collective-permute-start.5 = (f32[6,2,128]{2,1,0:T(2,128)S(1)}, f32[6,2,128]{2,1,0:T(2,128)S(1)}, u32[]{:S(2)}, u32[]{:S(2)}) collective-permute-start(f32[6,2,128]{2,1,0:T(2,128)S(1)} %get-tuple-element.74), channel_id=1, source_target_pairs={{64,0},{128,64},{192,128},{256,192},{320,256},{384,320},{448,384},... | collective-permute-start | bytes 18440 | tf_op jit(solution)/shard_map/ppermute | solution.py:35
  47.0 14.6 %collective-permute-start.4 = (f32[6,2,128]{2,1,0:T(2,128)S(1)}, f32[6,2,128]{2,1,0:T(2,128)S(1)}, u32[]{:S(2)}, u32[]{:S(2)}) collective-permute-start(f32[6,2,128]{2,1,0:T(2,128)S(1)} %get-tuple-element.73), channel_id=1, source_target_pairs={{0,64},{64,128},{128,192},{192,256},{256,320},{320,384},{384,448},... | collective-permute-start | bytes 18440 | tf_op jit(solution)/shard_map/ppermute | solution.py:34
  48.6 13.0 %all-to-all-start = ((f32[16,1,4]{2,1,0:T(1,128)}), f32[16,1,4]{2,1,0:T(1,128)S(1)}, u32[]{:S(2)}, u32[]{:S(2)}) async-start(f32[16,1,4]{2,1,0:T(1,128)} %bitcast.51), calls=%async_computation | async-start | bytes 16384 | tf_op jit(solution)/shard_map/all_to_all | solution.py:47
  61.8 12.1 %collective-permute-start.7 = (f32[6,20,2]{2,1,0:T(8,128)S(1)}, f32[6,20,2]{2,1,0:T(8,128)S(1)}, u32[]{:S(2)}, u32[]{:S(2)}) collective-permute-start(f32[6,20,2]{2,1,0:T(8,128)S(1)} %get-tuple-element.68), channel_id=1, source_target_pairs={{1,0},{2,1},{3,2},{4,3},{5,4},{6,5},{7,6},{8,7},{9,8},{10,9},{11,1... | collective-permute-start | bytes 2888 | tf_op jit(solution)/shard_map/ppermute | solution.py:35
  63.7 10.2 %collective-permute-start.6 = (f32[6,20,2]{2,1,0:T(8,128)S(1)}, f32[6,20,2]{2,1,0:T(8,128)S(1)}, u32[]{:S(2)}, u32[]{:S(2)}) collective-permute-start(f32[6,20,2]{2,1,0:T(8,128)S(1)} %get-tuple-element.67), channel_id=1, source_target_pairs={{0,1},{1,2},{2,3},{3,4},{4,5},{5,6},{6,7},{7,8},{8,9},{9,10},{10,1... | collective-permute-start | bytes 2888 | tf_op jit(solution)/shard_map/ppermute | solution.py:34
  67.8 16.9 %all-to-all-start.2 = ((f32[64,1,8]{2,1,0:T(1,128)}), f32[64,1,8]{2,1,0:T(1,128)S(1)}, u32[]{:S(2)}, u32[]{:S(2)}) async-start(f32[64,1,8]{2,1,0:T(1,128)} %broadcast_in_dim.64), calls=%async_computation.2 | async-start | bytes 65536 | tf_op jit(solution)/shard_map/all_to_all | solution.py:53
  74.5 10.3 %collective-permute-start.9 = (f32[6,2,128]{2,1,0:T(2,128)S(1)}, f32[6,2,128]{2,1,0:T(2,128)S(1)}, u32[]{:S(2)}, u32[]{:S(2)}) collective-permute-start(f32[6,2,128]{2,1,0:T(2,128)S(1)} %get-tuple-element.72), channel_id=1, source_target_pairs={{64,0},{128,64},{192,128},{256,192},{320,256},{384,320},{448,384},... | collective-permute-start | bytes 18440 | tf_op jit(solution)/shard_map/ppermute | solution.py:35
  75.7 9.0 %collective-permute-start.8 = (f32[6,2,128]{2,1,0:T(2,128)S(1)}, f32[6,2,128]{2,1,0:T(2,128)S(1)}, u32[]{:S(2)}, u32[]{:S(2)}) collective-permute-start(f32[6,2,128]{2,1,0:T(2,128)S(1)} %get-tuple-element.71), channel_id=1, source_target_pairs={{0,64},{64,128},{128,192},{192,256},{256,320},{320,384},{384,448},... | collective-permute-start | bytes 18440 | tf_op jit(solution)/shard_map/ppermute | solution.py:34
  84.9 5.9 %collective-permute-start.11 = (f32[6,20,2]{2,1,0:T(8,128)S(1)}, f32[6,20,2]{2,1,0:T(8,128)S(1)}, u32[]{:S(2)}, u32[]{:S(2)}) collective-permute-start(f32[6,20,2]{2,1,0:T(8,128)S(1)} %get-tuple-element.66), channel_id=1, source_target_pairs={{1,0},{2,1},{3,2},{4,3},{5,4},{6,5},{7,6},{8,7},{9,8},{10,9},{11,1... | collective-permute-start | bytes 2888 | tf_op jit(solution)/shard_map/ppermute | solution.py:35
  87.1 8.4 %collective-permute-start.10 = (f32[6,20,2]{2,1,0:T(8,128)S(1)}, f32[6,20,2]{2,1,0:T(8,128)S(1)}, u32[]{:S(2)}, u32[]{:S(2)}) collective-permute-start(f32[6,20,2]{2,1,0:T(8,128)S(1)} %get-tuple-element.65), channel_id=1, source_target_pairs={{0,1},{1,2},{2,3},{3,4},{4,5},{5,6},{6,7},{7,8},{8,9},{9,10},{10,1... | collective-permute-start | bytes 2888 | tf_op jit(solution)/shard_map/ppermute | solution.py:34
  (2 other events, 1.4 us)
where the time goes:
time: 99.2 us; the launch traced here: 97.3 us
  starting transfers between devices  58.5 us (59%)
  waiting for transfers between devices  25 us (25%)
  other arithmetic  7.78 us (8%)
  local copies, waits for them, and re-layouts  5.02 us (5%)
  between operations  1.05 us (1%)
    ppermute x6, starting transfers between devices, with_halo(): after = lax.ppermute(leading, axis, down)  32.2 us
    ppermute x6, waiting for transfers between devices, with_halo(): before = lax.ppermute(last, axis, up)  10.5 us
    ppermute x6, starting transfers between devices, with_halo(): before = lax.ppermute(last, axis, up)  10.4 us
    all_to_all x2, starting transfers between devices, sent_and_summed(): lax.all_to_all(pieces, axis, split_axis=0, concat_axis=0, tiled=True)  9.71 us
    all_to_all x1, waiting for transfers between devices, sent_to_all(): lax.all_to_all(jnp.broadcast_to(value[None], (length, *value.shape)), axi...  7.62 us
    all_to_all x2, waiting for transfers between devices, sent_and_summed(): lax.all_to_all(pieces, axis, split_axis=0, concat_axis=0, tiled=True)  6.86 us
    all_to_all x1, starting transfers between devices, sent_to_all(): lax.all_to_all(jnp.broadcast_to(value[None], (length, *value.shape)), axi...  6.09 us
    unnamed x24, local copies, waits for them, and re-layouts  2.72 us
  transfers between devices with their start and end apart: 15, of which 4 were waited for; matrix products, arithmetic and copies ran while one was open for 5% of the time, Pallas kernels for 0%

commit v1 on v0

v1 whole, which is shorter than its diff:
```python
import jax
import jax.numpy as jnp
from jax import lax
from jax.sharding import PartitionSpec as P

DEPTH_CLASSES = 5
VERTICAL_LEVELS = 7
SUBCYCLES = 3
SWEEPS = 2
BANDS_DEV = 4

FREEZE_POINT = -1.8
BASE_CONDUCT = 2.03
SALT_CONDUCT = 0.416
GROWTH_RATE = 0.02
STRENGTH_DECAY = 5.0
STRAIN_FLOOR = 0.0025

WIDTHS = (6, 6, 5, 5, 5, 5, 4, 4, 4, 4)


def columns_step(temp, depth, surf):
    scaled = 1.0 / (depth * depth)
    half = scaled * 0.5
    guess = temp
    for sweep in range(SWEEPS):
        conduct = [BASE_CONDUCT + SALT_CONDUCT / g for g in guess]
        coupling = [scaled * conduct[0]]
        for k in range(1, VERTICAL_LEVELS):
            coupling.append(half * (conduct[k - 1] + conduct[k]))
        coupling.append(scaled * conduct[VERTICAL_LEVELS - 1])
        ratio, passed = [], []
        for k in range(VERTICAL_LEVELS):
            source = temp[k]
            divisor = 1.0 + coupling[k] + coupling[k + 1]
            if k == 0:
                source = source + coupling[0] * surf
            else:
                divisor = divisor - coupling[k] * ratio[k - 1]
                source = source + coupling[k] * passed[k - 1]
            if k == VERTICAL_LEVELS - 1:
                source = source + coupling[VERTICAL_LEVELS] * FREEZE_POINT
            inverse = 1.0 / divisor
            ratio.append(coupling[k + 1] * inverse)
            passed.append(source * inverse)
        solved = list(passed)
        for k in range(VERTICAL_LEVELS - 2, -1, -1):
            solved[k] = passed[k] + ratio[k] * solved[k + 1]
        guess = solved
    return guess


def rows_exchange(planes):
    n = lax.axis_size("lat")
    up = [(i, i + 1) for i in range(n - 1)]
    down = [(i + 1, i) for i in range(n - 1)]
    last = jnp.concatenate([p[-w:] for p, w in zip(planes, WIDTHS)], axis=0)
    first = jnp.concatenate([p[:w] for p, w in zip(planes, WIDTHS)], axis=0)
    return lax.ppermute(last, "lat", up), lax.ppermute(first, "lat", down)


def rows_joined(planes, before, after):
    out, at = [], 0
    for p, w in zip(planes, WIDTHS):
        out.append(jnp.concatenate([before[at : at + w], p, after[at : at + w]], axis=0))
        at += w
    return out


def evened(p, rows):
    gap = (rows - p.shape[0]) // 2
    return jnp.pad(p, ((gap, gap), (0, 0))) if gap else p


def cols_exchange(planes):
    n = lax.axis_size("lon")
    right = [(i, (i + 1) % n) for i in range(n)]
    left = [((i + 1) % n, i) for i in range(n)]
    rows = planes[0].shape[0]
    last = jnp.concatenate([evened(p[:, -w:], rows) for p, w in zip(planes, WIDTHS)], axis=1)
    first = jnp.concatenate([evened(p[:, :w], rows) for p, w in zip(planes, WIDTHS)], axis=1)
    return lax.ppermute(last, "lon", right), lax.ppermute(first, "lon", left)


def cols_joined(planes, before, after):
    out, at = [], 0
    for p, w in zip(planes, WIDTHS):
        gap = (before.shape[0] - p.shape[0]) // 2
        rows = slice(gap, gap + p.shape[0])
        out.append(
            jnp.concatenate([before[rows, at : at + w], p, after[rows, at : at + w]], axis=1)
        )
        at += w
    return out


def trim(p, n):
    return p[n:-n, n:-n] if n else p


def east(p):
    return (p[1:-1, 2:] - p[1:-1, :-2]) * 0.5


def north(p):
    return (p[2:, 1:-1] - p[:-2, 1:-1]) * 0.5


def subcycles(planes):
    u, v, s1, s2, s12, strength, a, b, cx, cy = planes
    third = 1.0 / 1.5
    for step in range(SUBCYCLES):
        left = 2 * (SUBCYCLES - 1 - step)
        ue, un, ve, vn = east(u), north(u), east(v), north(v)
        divergence, tension, shearing = ue + vn, ue - vn, un + ve
        square = (
            divergence * divergence
            + (tension * tension + shearing * shearing) * 0.25
            + STRAIN_FLOOR
        )
        inverse = lax.rsqrt(square)
        pull = trim(strength, 2 * step) * inverse
        s1 = (s1 + 0.5 * pull * (divergence - square * inverse)) * third
        s2 = (s2 + 0.125 * pull * tension) * third
        s12 = (s12 + 0.0625 * pull * shearing) * third
        n11, n22 = 0.5 * (s1 + s2), 0.5 * (s1 - s2)
        px, py = east(n11) + north(s12), east(s12) + north(n22)
        n = 2 * step
        u = trim(a, n) * trim(u, 2) + trim(b, n) * px + trim(cx, n)
        v = trim(a, n) * trim(v, 2) + trim(b, n) * py + trim(cy, n)
        if step < SUBCYCLES - 1:
            s1, s2, s12 = trim(s1, 2), trim(s2, 2), trim(s12, 2)
        else:
            s1, s2, s12 = trim(s1, 1), trim(s2, 1), trim(s12, 1)
    return jnp.stack([u, v]), jnp.stack([s1, s2, s12])


def local(
    layer_temp,
    ice_depth_per_class,
    ice_area,
    surf_temp,
    seawater_thermal_input,
    velocity,
    stress,
    wind_stress,
    current,
    land_mask,
    ice_mask,
    band_index,
):
    rows, _, cols = layer_temp.shape
    lat_size, lon_size = lax.axis_size("lat"), lax.axis_size("lon")
    strip_ice = (ice_mask[0] == 1)[:, None, None]

    layers = layer_temp.reshape(rows, DEPTH_CLASSES, VERTICAL_LEVELS, cols)
    temp = [layers[:, :, k] for k in range(VERTICAL_LEVELS)]
    solved = columns_step(temp, ice_depth_per_class, surf_temp[:, None])
    bottom = solved[-1]
    regrown = (
        ice_depth_per_class
        + GROWTH_RATE * (BASE_CONDUCT + SALT_CONDUCT / bottom) * (FREEZE_POINT - bottom)
        / ice_depth_per_class
        - seawater_thermal_input[:, None]
    )
    thick_after = jnp.where(strip_ice, regrown, ice_depth_per_class)
    temp_after = jnp.where(
        strip_ice, jnp.stack(solved, axis=2).reshape(layer_temp.shape), layer_temp
    )

    row_total = jnp.sum(ice_area * thick_after, axis=(1, 2))
    bands = jnp.arange(BANDS_DEV * lat_size, dtype=jnp.int32)
    members = (band_index[:, None] == bands[None, :]).astype(jnp.float32)
    part_sum = jnp.sum(members * row_total[:, None], axis=0).reshape(lat_size, 1, BANDS_DEV)
    part_rows = jnp.sum(members, axis=0).reshape(lat_size, 1, BANDS_DEV)
    parts = jnp.concatenate([part_sum, part_rows], axis=2)

    volume_start = jnp.sum(ice_area * ice_depth_per_class, axis=1)
    coverage = jnp.sum(ice_area, axis=1)
    strength = volume_start * jnp.exp(-STRENGTH_DECAY * (1.0 - coverage))
    a = land_mask.astype(jnp.float32) * (1.0 / 1.5)
    half = 0.5 * a
    b = half / (1.0 + volume_start)
    push = wind_stress + current
    planes = [
        velocity[0], velocity[1], stress[0], stress[1], stress[2],
        strength, a, b, half * push[0], half * push[1],
    ]

    parts, planes = lax.optimization_barrier((parts, planes))
    arrived = lax.all_to_all(parts, "lat", 0, 0, tiled=True)
    before, after = rows_exchange(planes)
    total = jnp.sum(arrived, axis=(0, 1))
    share = total[:BANDS_DEV] / (total[BANDS_DEV:] * float(cols * lon_size))
    spread = jnp.broadcast_to(share[None, None], (lon_size, 1, BANDS_DEV))
    spread, before, after = lax.optimization_barrier((spread, before, after))
    shares = lax.all_to_all(spread, "lon", 0, 0, tiled=True)
    planes = rows_joined(planes, before, after)
    before, after = cols_exchange(planes)
    planes = cols_joined(planes, before, after)
    moving, stresses = subcycles(planes)
    zonal_volume = jnp.sum(shares, axis=(0, 1))
    return (temp_after, thick_after, moving, stresses, zonal_volume)


def solution(mesh):
    return jax.shard_map(
        local,
        mesh=mesh,
        in_specs=(
            P("lat", None, "lon"),
            P("lat", None, "lon"),
            P("lat", None, "lon"),
            P("lat", "lon"),
            P("lat", "lon"),
            P(None, "lat", "lon"),
            P(None, "lat", "lon"),
            P(None, "lat", "lon"),
            P(None, "lat", "lon"),
            P("lat", "lon"),
            P("lon", "lat"),
            P("lat"),
        ),
        out_specs=(
            P("lat", None, "lon"),
            P("lat", None, "lon"),
            P(None, "lat", "lon"),
            P(None, "lat", "lon"),
            P("lat"),
        ),
        check_vma=False,
    )
```

time: 99.2 us -> 67.9 us (0.68)
  the two profiles are of different devices: /device:TPU:1 before, /device:TPU:49 now
where the time goes in v1:
time: 67.9 us; the launch traced here: 67.2 us
  starting transfers between devices  41.7 us (61%)
  waiting for transfers between devices  10.8 us (16%)
  other arithmetic  8.17 us (12%)
  local copies, waits for them, and re-layouts  5.38 us (8%)
  between operations  1.11 us (2%)
    all_to_all x1, starting transfers between devices, local(): arrived = lax.all_to_all(parts, 'lat', 0, 0, tiled=True)  16.1 us
    ppermute x2, starting transfers between devices, cols_exchange(): return (lax.ppermute(last, 'lon', right), lax.ppermute(first, 'lon', left))  13.9 us
    all_to_all x1, waiting for transfers between devices, local(): shares = lax.all_to_all(spread, 'lon', 0, 0, tiled=True)  6.89 us
    ppermute x2, starting transfers between devices, rows_exchange(): return (lax.ppermute(last, 'lat', up), lax.ppermute(first, 'lat', down))  6.46 us
    all_to_all x1, starting transfers between devices, local(): shares = lax.all_to_all(spread, 'lon', 0, 0, tiled=True)  5.19 us
    ppermute x2, waiting for transfers between devices, rows_exchange(): return (lax.ppermute(last, 'lat', up), lax.ppermute(first, 'lat', down))  3.95 us
    unnamed x25, local copies, waits for them, and re-layouts  2.16 us
  transfers between devices with their start and end apart: 6, of which 2 were waited for; matrix products, arithmetic and copies ran while one was open for 4% of the time, Pallas kernels for 0%

profile of v1, /device:TPU:49, one launch (start us, length us, event | category | flops | bytes accessed | tf_op | source)
XLA Modules:
  0.0 67.2 jit_solution(18339184496079491381)
XLA Ops:
  0.6 0.7 compare_bitcast_fusion
  1.3 1.1 %add_multiply_fusion.15 = (f32[16,5,128]{2,0,1:T(8,128)S(1)}, f32[16,5,128]{2,0,1:T(8,128)S(1)}, f32[16,5,128]{2,0,1:T(8,128)S(1)}, f32[16,5,128]{2,0,1:T(8,128)...) fusion(f32[16,5,7,128]{3,0,2,1:T(8,128)} %bitcast.247, ...), kind=kLoop, calls=%fused_computation.66 | loop fusion | flops 696320 | bytes 622592 | tf_op jit(solution)/shard_map/mul | solution.py:45
  2.5 0.7 copy-done.3
  3.2 1.0 %fusion.64 = (f32[16,128]{1,0:T(8,128)S(1)}, f32[16]{0:T(128)S(1)}, f32[16,128]{1,0:T(8,128)S(1)}, f32[16,5,128]{2,0,1:T(8,128)}, f32[16,5,128]{2,0,1:T(8,128)S(...) fusion(f32[16,5,128]{2,0,1:T(8,128)S(1)} %copy-done.3, ...), kind=kLoop, calls=%fused_computation.238 | loop fusion | flops 1511408 | bytes 1179728 | tf_op jit(solution)/shard_map/reduce_sum | solution.py:179
  4.5 0.7 %pad_maximum_fusion.19 = f32[16,1,8]{2,0,1:T(8,128)} fusion(f32[16,1,4]{2,0,1:T(8,128)S(1)} %reshape.39, f32[16,1,4]{2,0,1:T(8,128)S(1)} %reshape.38), kind=kLoop, calls=%fused_computation.223 | loop fusion | flops 128 | bytes 1024 | tf_op jit(solution)/shard_map/concatenate | solution.py:176
  5.2 0.7 %copy-done.6 = f32[2,16,128]{2,1,0:T(8,128)S(1)} copy-done((f32[2,16,128]{2,1,0:T(8,128)S(1)}, f32[2,16,128]{2,1,0:T(8,128)}, u32[]{:S(2)}) %copy-start.6) | copy-done | bytes 16408
  5.9 0.7 %copy-done.9 = s32[16,128]{1,0:T(8,128)S(1)} copy-done((s32[16,128]{1,0:T(8,128)S(1)}, s32[16,128]{1,0:T(8,128)}, u32[]{:S(2)}) %copy-start.9) | copy-done | bytes 8216
  6.7 16.1 %all-to-all-start = ((f32[16,1,8]{2,1,0:T(1,128)}), f32[16,1,8]{2,1,0:T(1,128)S(1)}, u32[]{:S(2)}, u32[]{:S(2)}) async-start(f32[16,1,8]{2,1,0:T(1,128)} %bitcast.24), calls=%async_computation | async-start | bytes 16384 | tf_op jit(solution)/shard_map/all_to_all | solution.py:191
  22.9 0.3 concatenate.76
  23.2 4.5 %collective-permute-start = (f32[48,128]{1,0:T(8,128)S(1)}, f32[48,128]{1,0:T(8,128)S(1)}, u32[]{:S(2)}, u32[]{:S(2)}) collective-permute-start(f32[48,128]{1,0:T(8,128)S(1)} %concatenate.76), channel_id=1, source_target_pairs={{0,64},{64,128},{128,192},{192,256},{256,320},{320,384},{384,448},... | collective-permute-start | bytes 73736 | tf_op jit(solution)/shard_map/ppermute | solution.py:59
  27.8 0.3 concatenate.77
  28.1 1.9 %collective-permute-start.1 = (f32[48,128]{1,0:T(8,128)S(1)}, f32[48,128]{1,0:T(8,128)S(1)}, u32[]{:S(2)}, u32[]{:S(2)}) collective-permute-start(f32[48,128]{1,0:T(8,128)S(1)} %concatenate.77), channel_id=1, source_target_pairs={{64,0},{128,64},{192,128},{256,192},{320,256},{384,320},{448,384},... | collective-permute-start | bytes 73736 | tf_op jit(solution)/shard_map/ppermute | solution.py:59
  30.5 4.0 %collective-permute-done.1 = f32[48,128]{1,0:T(8,128)S(1)} collective-permute-done((f32[48,128]{1,0:T(8,128)S(1)}, f32[48,128]{1,0:T(8,128)S(1)}, u32[]{:S(2)}, u32[]{:S(2)}) %collective-permute-start.1) | collective-permute-done | bytes 24608 | tf_op jit(solution)/shard_map/ppermute | solution.py:59
  34.5 0.6 broadcast_in_dim.20
  36.2 11.0 %collective-permute-start.3 = (f32[28,48]{1,0:T(8,128)S(1)}, f32[28,48]{1,0:T(8,128)S(1)}, u32[]{:S(2)}, u32[]{:S(2)}) collective-permute-start(f32[28,48]{1,0:T(8,128)S(1)} %concatenate.89), channel_id=1, source_target_pairs={{1,0},{2,1},{3,2},{4,3},{5,4},{6,5},{7,6},{8,7},{9,8},{10,9},{11,1... | collective-permute-start | bytes 16136 | tf_op jit(solution)/shard_map/ppermute | solution.py:82
  47.2 5.2 %all-to-all-start.1 = ((f32[64,1,4]{2,1,0:T(1,128)}), f32[64,1,4]{2,1,0:T(1,128)S(1)}, u32[]{:S(2)}, u32[]{:S(2)}) async-start(f32[64,1,4]{2,1,0:T(1,128)} %broadcast_in_dim.20), calls=%async_computation.1 | async-start | bytes 65536 | tf_op jit(solution)/shard_map/all_to_all | solution.py:197
  52.4 0.8 %bitcast_select_fusion = f32[16,35,128]{2,0,1:T(8,128)} fusion(f32[16,35,128]{2,0,1:T(8,128)S(1)} %copy-done, f32[16,5,7,128]{3,0,2,1:T(8,128)S(1)} %copy.46, pred[16]{0:T(512)(128)(4,1)S(1)} %compare_bitcast_fusion), kind=kLoop, calls=%fused_computation | loop fusion | flops 71680 | bytes 860176 | tf_op jit(solution)/shard_map/jit(_where)/select_n | solution.py:167
  53.4 2.9 %collective-permute-start.2 = (f32[28,48]{1,0:T(8,128)S(1)}, f32[28,48]{1,0:T(8,128)S(1)}, u32[]{:S(2)}, u32[]{:S(2)}) collective-permute-start(f32[28,48]{1,0:T(8,128)S(1)} %concatenate.88), channel_id=1, source_target_pairs={{0,1},{1,2},{2,3},{3,4},{4,5},{5,6},{6,7},{7,8},{8,9},{9,10},{10,1... | collective-permute-start | bytes 16136 | tf_op jit(solution)/shard_map/ppermute | solution.py:82
  56.3 6.9 %all-to-all-done.1 = f32[64,1,4]{2,1,0:T(1,128)S(1)} async-done(((f32[64,1,4]{2,1,0:T(1,128)}), f32[64,1,4]{2,1,0:T(1,128)S(1)}, u32[]{:S(2)}, u32[]{:S(2)}) %all-to-all-start.1) | async-done | bytes 1056 | tf_op jit(solution)/shard_map/all_to_all | solution.py:197
  63.2 0.6 reduce_sum.69
  64.3 0.2 add_multiply_fusion.24
  65.3 0.1 slice_add_fusion.3
  66.0 0.6 pad_maximum_fusion.14
  66.6 0.6 pad_maximum_fusion.7
  (115 shorter events, 3.8 us)
Async XLA Ops:
  1.3 1.1 %copy-start = (f32[16,35,128]{2,0,1:T(8,128)S(1)}, f32[16,35,128]{2,0,1:T(8,128)}, u32[]{:S(2)}) copy-start(f32[16,35,128]{2,0,1:T(8,128)} %param.12) | copy-start | bytes 860164
  1.3 1.1 %copy-start.1 = (f32[16,5,128]{2,0,1:T(8,128)S(1)}, f32[16,5,128]{2,0,1:T(8,128)}, u32[]{:S(2)}) copy-start(f32[16,5,128]{2,0,1:T(8,128)} %param.13) | copy-start | bytes 122884
  2.4 0.8 %copy-start.3 = (f32[16,5,128]{2,0,1:T(8,128)S(1)}, f32[16,5,128]{2,0,1:T(8,128)}, u32[]{:S(2)}) copy-start(f32[16,5,128]{2,0,1:T(8,128)} %param.14) | copy-start | bytes 122884
  2.4 0.8 %copy-start.8 = (f32[16,128]{1,0:T(8,128)S(1)}, f32[16,128]{1,0:T(8,128)}, u32[]{:S(2)}) copy-start(f32[16,128]{1,0:T(8,128)} %param.16) | copy-start | bytes 24580
  2.5 0.7 %copy-start.2 = (f32[16,128]{1,0:T(8,128)S(1)}, f32[16,128]{1,0:T(8,128)}, u32[]{:S(2)}) copy-start(f32[16,128]{1,0:T(8,128)} %param.15) | copy-start | bytes 24580
  3.2 1.0 %copy-start.10 = (s32[16]{0:T(128)S(1)}, s32[16]{0:T(128)}, u32[]{:S(2)}) copy-start(s32[16]{0:T(128)} %param.23) | copy-start | bytes 196
  4.2 1.0 %copy-start.4 = (f32[3,16,128]{2,1,0:T(8,128)S(1)}, f32[3,16,128]{2,1,0:T(8,128)}, u32[]{:S(2)}) copy-start(f32[3,16,128]{2,1,0:T(8,128)} %param.18) | copy-start | bytes 73732
  4.4 0.8 %copy-start.5 = (f32[2,16,128]{2,1,0:T(8,128)S(1)}, f32[2,16,128]{2,1,0:T(8,128)}, u32[]{:S(2)}) copy-start(f32[2,16,128]{2,1,0:T(8,128)} %param.17) | copy-start | bytes 49156
  5.2 0.7 %copy-start.6 = (f32[2,16,128]{2,1,0:T(8,128)S(1)}, f32[2,16,128]{2,1,0:T(8,128)}, u32[]{:S(2)}) copy-start(f32[2,16,128]{2,1,0:T(8,128)} %param.19) | copy-start | bytes 49156
  5.2 0.7 %copy-start.7 = (f32[2,16,128]{2,1,0:T(8,128)S(1)}, f32[2,16,128]{2,1,0:T(8,128)}, u32[]{:S(2)}) copy-start(f32[2,16,128]{2,1,0:T(8,128)} %param.20) | copy-start | bytes 49156
  5.9 0.7 %copy-start.9 = (s32[16,128]{1,0:T(8,128)S(1)}, s32[16,128]{1,0:T(8,128)}, u32[]{:S(2)}) copy-start(s32[16,128]{1,0:T(8,128)} %param.21) | copy-start | bytes 24580
  6.7 23.8 %all-to-all-start = ((f32[16,1,8]{2,1,0:T(1,128)}), f32[16,1,8]{2,1,0:T(1,128)S(1)}, u32[]{:S(2)}, u32[]{:S(2)}) async-start(f32[16,1,8]{2,1,0:T(1,128)} %bitcast.24), calls=%async_computation | async-start | bytes 16384 | tf_op jit(solution)/shard_map/all_to_all | solution.py:191
  23.2 7.3 %collective-permute-start = (f32[48,128]{1,0:T(8,128)S(1)}, f32[48,128]{1,0:T(8,128)S(1)}, u32[]{:S(2)}, u32[]{:S(2)}) collective-permute-start(f32[48,128]{1,0:T(8,128)S(1)} %concatenate.76), channel_id=1, source_target_pairs={{0,64},{64,128},{128,192},{192,256},{256,320},{320,384},{384,448},... | collective-permute-start | bytes 73736 | tf_op jit(solution)/shard_map/ppermute | solution.py:59
  28.1 6.3 %collective-permute-start.1 = (f32[48,128]{1,0:T(8,128)S(1)}, f32[48,128]{1,0:T(8,128)S(1)}, u32[]{:S(2)}, u32[]{:S(2)}) collective-permute-start(f32[48,128]{1,0:T(8,128)S(1)} %concatenate.77), channel_id=1, source_target_pairs={{64,0},{128,64},{192,128},{256,192},{320,256},{384,320},{448,384},... | collective-permute-start | bytes 73736 | tf_op jit(solution)/shard_map/ppermute | solution.py:59
  36.2 27.6 %collective-permute-start.3 = (f32[28,48]{1,0:T(8,128)S(1)}, f32[28,48]{1,0:T(8,128)S(1)}, u32[]{:S(2)}, u32[]{:S(2)}) collective-permute-start(f32[28,48]{1,0:T(8,128)S(1)} %concatenate.89), channel_id=1, source_target_pairs={{1,0},{2,1},{3,2},{4,3},{5,4},{6,5},{7,6},{8,7},{9,8},{10,9},{11,1... | collective-permute-start | bytes 16136 | tf_op jit(solution)/shard_map/ppermute | solution.py:82
  47.2 16.0 %all-to-all-start.1 = ((f32[64,1,4]{2,1,0:T(1,128)}), f32[64,1,4]{2,1,0:T(1,128)S(1)}, u32[]{:S(2)}, u32[]{:S(2)}) async-start(f32[64,1,4]{2,1,0:T(1,128)} %broadcast_in_dim.20), calls=%async_computation.1 | async-start | bytes 65536 | tf_op jit(solution)/shard_map/all_to_all | solution.py:197
  53.4 10.5 %collective-permute-start.2 = (f32[28,48]{1,0:T(8,128)S(1)}, f32[28,48]{1,0:T(8,128)S(1)}, u32[]{:S(2)}, u32[]{:S(2)}) collective-permute-start(f32[28,48]{1,0:T(8,128)S(1)} %concatenate.88), channel_id=1, source_target_pairs={{0,1},{1,2},{2,3},{3,4},{4,5},{5,6},{6,7},{7,8},{8,9},{9,10},{10,1... | collective-permute-start | bytes 16136 | tf_op jit(solution)/shard_map/ppermute | solution.py:82

commit v2 on v1

v2 whole, which is shorter than its diff:
```python
import jax
import jax.numpy as jnp
from jax import lax
from jax.experimental import pallas as pl
from jax.experimental.pallas import tpu as pltpu
from jax.sharding import PartitionSpec as P

DEPTH_CLASSES = 5
VERTICAL_LEVELS = 7
SUBCYCLES = 3
SWEEPS = 2
BANDS_DEV = 4

FREEZE_POINT = -1.8
BASE_CONDUCT = 2.03
SALT_CONDUCT = 0.416
GROWTH_RATE = 0.02
STRENGTH_DECAY = 5.0
STRAIN_FLOOR = 0.0025

PLANES = 10
EDGE = 8
WIDTH = 6
THIRD = 1.0 / 1.5


def columns_step(temp, depth, surf):
    scaled = 1.0 / (depth * depth)
    half = scaled * 0.5
    guess = temp
    for sweep in range(SWEEPS):
        conduct = [BASE_CONDUCT + SALT_CONDUCT / g for g in guess]
        coupling = [scaled * conduct[0]]
        for k in range(1, VERTICAL_LEVELS):
            coupling.append(half * (conduct[k - 1] + conduct[k]))
        coupling.append(scaled * conduct[VERTICAL_LEVELS - 1])
        ratio, passed = [], []
        for k in range(VERTICAL_LEVELS):
            source = temp[k]
            divisor = 1.0 + coupling[k] + coupling[k + 1]
            if k == 0:
                source = source + coupling[0] * surf
            else:
                divisor = divisor - coupling[k] * ratio[k - 1]
                source = source + coupling[k] * passed[k - 1]
            if k == VERTICAL_LEVELS - 1:
                source = source + coupling[VERTICAL_LEVELS] * FREEZE_POINT
            inverse = 1.0 / divisor
            ratio.append(coupling[k + 1] * inverse)
            passed.append(source * inverse)
        solved = list(passed)
        for k in range(VERTICAL_LEVELS - 2, -1, -1):
            solved[k] = passed[k] + ratio[k] * solved[k + 1]
        guess = solved
    return guess


def columns_kernel(*refs):
    n = 12
    given, outs, here, sems = refs[:n], refs[n : n + 5], refs[n + 5 : n + 5 + n], refs[-1]
    copies = [pltpu.make_async_copy(a, b, sems.at[i]) for i, (a, b) in enumerate(zip(given, here))]
    for copy in copies:
        copy.start()
    for copy in copies:
        copy.wait()
    columns_body(*here, *outs)


def columns_body(
    temp_ref, depth_ref, area_ref, surf_ref, sea_ref, velocity_ref, stress_ref, wind_ref, current_ref,
    land_ref, ice_ref, band_ref, temp_out, thick_out, parts_out, first_out, last_out,
):
    rows = surf_ref.shape[0]
    depth, area = depth_ref[...], area_ref[...]

    volume = jnp.sum(area * depth, axis=0)
    coverage = jnp.sum(area, axis=0)
    a = land_ref[...].astype(jnp.float32) * THIRD
    half = 0.5 * a
    planes = (
        velocity_ref[0], velocity_ref[1], stress_ref[0], stress_ref[1], stress_ref[2],
        volume * jnp.exp(-STRENGTH_DECAY * (1.0 - coverage)),
        a, half / (1.0 + volume),
        half * (wind_ref[0] + current_ref[0]), half * (wind_ref[1] + current_ref[1]),
    )
    for f, plane in enumerate(planes):
        first_out[f] = plane[:EDGE]
        last_out[f] = plane[rows - EDGE :]

    temp = [
        jnp.stack([temp_ref[c * VERTICAL_LEVELS + k] for c in range(DEPTH_CLASSES)])
        for k in range(VERTICAL_LEVELS)
    ]
    solved = columns_step(temp, depth, surf_ref[...][None])
    bottom = solved[-1]
    regrown = (
        depth
        + GROWTH_RATE * (BASE_CONDUCT + SALT_CONDUCT / bottom) * (FREEZE_POINT - bottom) / depth
        - sea_ref[...][None]
    )
    square = (rows, rows)
    eye = lax.broadcasted_iota(jnp.int32, square, 0) == lax.broadcasted_iota(jnp.int32, square, 1)
    ice = jnp.broadcast_to(ice_ref[...].astype(jnp.float32), square)
    ice = jnp.sum(jnp.where(eye, ice, 0.0), axis=1, keepdims=True)
    ice = jnp.broadcast_to(ice, surf_ref.shape) == 1.0
    thick = [jnp.where(ice, regrown[c], depth[c]) for c in range(DEPTH_CLASSES)]
    after = area[0] * thick[0]
    for c in range(1, DEPTH_CLASSES):
        after = after + area[c] * thick[c]
    for c in range(DEPTH_CLASSES):
        thick_out[c] = thick[c]
        for k in range(VERTICAL_LEVELS):
            temp_out[c * VERTICAL_LEVELS + k] = jnp.where(ice, solved[k][c], temp[k][c])

    owners, _, entries = parts_out.shape
    total = jnp.broadcast_to(jnp.sum(after, axis=1, keepdims=True), (rows, entries))
    entry = lax.broadcasted_iota(jnp.int32, (owners, entries), 1)
    band = BANDS_DEV * lax.broadcasted_iota(jnp.int32, (owners, entries), 0) + entry % BANDS_DEV
    parts = jnp.zeros((owners, entries), jnp.float32)
    for r in range(rows):
        value = jnp.where(entry < BANDS_DEV, jnp.broadcast_to(total[r : r + 1], parts.shape), 1.0)
        parts = parts + jnp.where(band == band_ref[r], value, 0.0)
    parts_out[...] = parts[:, None, :]


def window(f, first_ref, last_ref, before_ref, after_ref):
    return jnp.concatenate([first_ref[f], last_ref[f], after_ref[f], before_ref[f]], axis=0)


def lanes_of(shape):
    return lax.broadcasted_iota(jnp.int32, shape, 1)


def pack_kernel(first_ref, last_ref, before_ref, after_ref, right_out, left_out):
    cols = right_out.shape[1]
    lanes = lanes_of(right_out.shape)
    right = jnp.zeros(right_out.shape, jnp.float32)
    left = jnp.zeros(right_out.shape, jnp.float32)
    for f in range(PLANES):
        plane = window(f, first_ref, last_ref, before_ref, after_ref)
        at = f * WIDTH
        here = (lanes >= at) & (lanes < at + WIDTH)
        right = jnp.where(here, pltpu.roll(plane, (at + WIDTH) % cols, 1), right)
        left = jnp.where(here, pltpu.roll(plane, at, 1) if at else plane, left)
    right_out[...] = right
    left_out[...] = left


def east(p):
    n = p.shape[1]
    return (pltpu.roll(p, n - 1, 1) - pltpu.roll(p, 1, 1)) * 0.5


def north(p):
    n = p.shape[0]
    return (pltpu.roll(p, n - 1, 0) - pltpu.roll(p, 1, 0)) * 0.5


def subcycles_kernel(
    first_ref, last_ref, before_ref, after_ref, west_ref, east_ref, velocity_out, stress_out
):
    rows, cols = velocity_out.shape[1:]
    west, onward = west_ref[...], east_ref[...]
    lanes = lanes_of(west.shape)
    fields = []
    for f in range(PLANES):
        at = f * WIDTH
        near = pltpu.roll(onward, cols - at, 1) if at else onward
        far = pltpu.roll(west, cols - WIDTH - at, 1)
        side = jnp.where(lanes < WIDTH, near, jnp.where(lanes >= cols - WIDTH, far, 0.0))
        plane = window(f, first_ref, last_ref, before_ref, after_ref)
        fields.append(jnp.concatenate([plane, side], axis=1))
    u, v, s1, s2, s12, strength, a, b, cx, cy = fields
    for _ in range(SUBCYCLES):
        ue, un, ve, vn = east(u), north(u), east(v), north(v)
        divergence, tension, shearing = ue + vn, ue - vn, un + ve
        square = (
            divergence * divergence
            + (tension * tension + shearing * shearing) * 0.25
            + STRAIN_FLOOR
        )
        inverse = lax.rsqrt(square)
        pull = strength * inverse
        s1 = (s1 + 0.5 * pull * (divergence - square * inverse)) * THIRD
        s2 = (s2 + 0.125 * pull * tension) * THIRD
        s12 = (s12 + 0.0625 * pull * shearing) * THIRD
        n11, n22 = 0.5 * (s1 + s2), 0.5 * (s1 - s2)
        u = a * u + b * (east(n11) + north(s12)) + cx
        v = a * v + b * (east(s12) + north(n22)) + cy
    velocity_out[0] = u[:rows, :cols]
    velocity_out[1] = v[:rows, :cols]
    stress_out[0] = s1[:rows, :cols]
    stress_out[1] = s2[:rows, :cols]
    stress_out[2] = s12[:rows, :cols]


def call(kernel, outs, flops, fetch=False):
    def run(*args):
        space = pltpu.HBM if fetch else pltpu.VMEM
        scratch = []
        if fetch:
            scratch = [pltpu.VMEM(a.shape, a.dtype) for a in args[:-1]]
            scratch += [pltpu.SMEM(args[-1].shape, jnp.int32), pltpu.SemaphoreType.DMA((len(args),))]
        return pl.pallas_call(
            kernel,
            out_shape=[jax.ShapeDtypeStruct(shape, jnp.float32) for shape in outs],
            in_specs=[pl.BlockSpec(memory_space=space)] * len(args),
            out_specs=[pl.BlockSpec(memory_space=pltpu.VMEM)] * len(outs),
            scratch_shapes=scratch,
            compiler_params=pltpu.CompilerParams(vmem_limit_bytes=(60 if fetch else 8) << 20),
            cost_estimate=pl.CostEstimate(flops=flops, bytes_accessed=flops // 8, transcendentals=0),
        )(*args)

    return run


def local(
    layer_temp,
    ice_depth_per_class,
    ice_area,
    surf_temp,
    seawater_thermal_input,
    velocity,
    stress,
    wind_stress,
    current,
    land_mask,
    ice_mask,
    band_index,
):
    rows, levels, cols = layer_temp.shape
    lat_size, lon_size = lax.axis_size("lat"), lax.axis_size("lon")
    half = (PLANES, EDGE, cols)
    swap = lambda x: jnp.transpose(x, (1, 0, 2))
    temp_after, thick_after, parts, first, last = call(
        columns_kernel,
        [(levels, rows, cols), (DEPTH_CLASSES, rows, cols), (lat_size, 1, 2 * BANDS_DEV), half, half],
        4_000_000,
        fetch=True,
    )(
        swap(layer_temp), swap(ice_depth_per_class), swap(ice_area), surf_temp,
        seawater_thermal_input, velocity, stress, wind_stress, current, land_mask, ice_mask, band_index,
    )
    arrived = lax.all_to_all(parts, "lat", 0, 0, tiled=True)
    before = lax.ppermute(last, "lat", [(i, i + 1) for i in range(lat_size - 1)])
    after = lax.ppermute(first, "lat", [(i + 1, i) for i in range(lat_size - 1)])

    total = jnp.sum(arrived, axis=(0, 1))
    share = total[:BANDS_DEV] / (total[BANDS_DEV:] * float(cols * lon_size))
    share = jnp.pad(share, (0, cols - BANDS_DEV))
    spread = jnp.broadcast_to(share[None, None], (lon_size, 1, cols))
    spread, before, after = lax.optimization_barrier((spread, before, after))
    shares = lax.all_to_all(spread, "lon", 0, 0, tiled=True)

    packed = (4 * EDGE, cols)
    right, left = call(pack_kernel, [packed, packed], 500_000)(first, last, before, after)
    west = lax.ppermute(right, "lon", [(i, (i + 1) % lon_size) for i in range(lon_size)])
    onward = lax.ppermute(left, "lon", [((i + 1) % lon_size, i) for i in range(lon_size)])
    moving, stresses = call(
        subcycles_kernel, [(2, rows, cols), (3, rows, cols)], 2_000_000
    )(first, last, before, after, west, onward)
    zonal_volume = jnp.sum(shares[:, :, :BANDS_DEV], axis=(0, 1))
    return (swap(temp_after), swap(thick_after), moving, stresses, zonal_volume)


def solution(mesh):
    return jax.shard_map(
        local,
        mesh=mesh,
        in_specs=(
            P("lat", None, "lon"),
            P("lat", None, "lon"),
            P("lat", None, "lon"),
            P("lat", "lon"),
            P("lat", "lon"),
            P(None, "lat", "lon"),
            P(None, "lat", "lon"),
            P(None, "lat", "lon"),
            P(None, "lat", "lon"),
            P("lat", "lon"),
            P("lon", "lat"),
            P("lat"),
        ),
        out_specs=(
            P("lat", None, "lon"),
            P("lat", None, "lon"),
            P(None, "lat", "lon"),
            P(None, "lat", "lon"),
            P("lat"),
        ),
        check_vma=False,
    )
```

time: 67.9 us -> 55.5 us (0.82)
  the two profiles are of different devices: /device:TPU:49 before, /device:TPU:72 now
where the time goes in v2:
time: 55.5 us; the launch traced here: 55.1 us
  starting transfers between devices  43.6 us (79%)
  waiting for transfers between devices  5.92 us (11%)
  Pallas kernels  3.6 us (6%)
  between operations  0.73 us (1%)
  other arithmetic  0.71 us (1%)
  local copies, waits for them, and re-layouts  0.64 us (1%)
    all_to_all x1, starting transfers between devices, local(): shares = lax.all_to_all(spread, 'lon', 0, 0, tiled=True)  22.8 us
    all_to_all x1, starting transfers between devices, local(): arrived = lax.all_to_all(parts, 'lat', 0, 0, tiled=True)  7.24 us
    ppermute x1, starting transfers between devices, local(): lax.ppermute(left, 'lon', [((i + 1) % lon_size, i) for i in range(lon_siz...  5.78 us
    ppermute x1, waiting for transfers between devices, local(): lax.ppermute(last, 'lat', [(i, i + 1) for i in range(lat_size - 1)])  4.5 us
    pallas_call x3, Pallas kernels, run(): pl.pallas_call(kernel, out_shape=[jax.ShapeDtypeStruct(shape, jnp.float32...  3.6 us
    ppermute x1, starting transfers between devices, local(): lax.ppermute(right, 'lon', [(i, (i + 1) % lon_size) for i in range(lon_si...  3.38 us
    ppermute x1, starting transfers between devices, local(): lax.ppermute(first, 'lat', [(i + 1, i) for i in range(lat_size - 1)])  2.21 us
    ppermute x1, starting transfers between devices, local(): lax.ppermute(last, 'lat', [(i, i + 1) for i in range(lat_size - 1)])  2.1 us
  transfers between devices with their start and end apart: 6, of which 2 were waited for; matrix products, arithmetic and copies ran while one was open for 0% of the time, Pallas kernels for 3%

profile of v2, /device:TPU:72, one launch (start us, length us, event | category | flops | bytes accessed | tf_op | source)
XLA Modules:
  0.0 55.1 jit_solution(13827373048868018115)
XLA Ops:
  0.6 2.2 %shard_map.155 = (f32[35,16,128]{2,1,0:T(8,128)}, f32[5,16,128]{2,1,0:T(8,128)}, f32[16,1,8]{2,1,0:T(1,128)}, f32[10,8,128]{2,1,0:T(8,128)}, f32[10,8,128]{2,1,0:T(8,128)}) custom-call(f32[35,16,128]{2,1,0:T(8,128)} %bitcast.5, f32[5,16,128]{2,1,0:T(8,128)} %bitcast.6, f32[5,16,128]{2,1,0:T(8,128)} %bitcast.7, f32[16,128]{1,0:T(8,128)} %refs_3_.1, ...), custom_call_target="tpu_custom_call" | custom-call | flops 4000000 | bytes 500000 | tf_op jit(solution)/shard_map/pallas_call | solution.py:204
  2.8 7.2 %all-to-all-start = ((f32[16,1,8]{2,1,0:T(1,128)}), f32[16,1,8]{2,1,0:T(1,128)S(1)}, u32[]{:S(2)}, u32[]{:S(2)}) async-start(f32[16,1,8]{2,1,0:T(1,128)} %get-tuple-element.21), calls=%async_computation | async-start | bytes 16384 | tf_op jit(solution)/shard_map/all_to_all | solution.py:244
  10.1 2.2 %collective-permute-start.1 = (f32[10,8,128]{2,1,0:T(8,128)}, f32[10,8,128]{2,1,0:T(8,128)S(1)}, u32[]{:S(2)}, u32[]{:S(2)}) collective-permute-start(f32[10,8,128]{2,1,0:T(8,128)} %get-tuple-element.19.first_ref), channel_id=1, source_target_pairs={{64,0},{128,64},{192,128},{256,192},{320,256},{384,320},{448,384},... | collective-permute-start | bytes 122888 | tf_op jit(solution)/shard_map/ppermute | solution.py:246
  12.3 2.1 %collective-permute-start = (f32[10,8,128]{2,1,0:T(8,128)}, f32[10,8,128]{2,1,0:T(8,128)S(1)}, u32[]{:S(2)}, u32[]{:S(2)}) collective-permute-start(f32[10,8,128]{2,1,0:T(8,128)} %get-tuple-element.20.last_ref), channel_id=1, source_target_pairs={{0,64},{64,128},{128,192},{192,256},{256,320},{320,384},{384,448},... | collective-permute-start | bytes 122888 | tf_op jit(solution)/shard_map/ppermute | solution.py:245
  14.4 0.0 all-to-all-done
  14.5 0.1 multiply_divide_fusion
  14.5 0.0 collective-permute-done.1.after_ref
  14.5 4.5 %collective-permute-done.before_ref = f32[10,8,128]{2,1,0:T(8,128)S(1)} collective-permute-done((f32[10,8,128]{2,1,0:T(8,128)}, f32[10,8,128]{2,1,0:T(8,128)S(1)}, u32[]{:S(2)}, u32[]{:S(2)}) %collective-permute-start) | collective-permute-done | bytes 40992 | tf_op jit(solution)/shard_map/ppermute | solution.py:245
  19.0 0.0 copy-start.1
  19.0 0.6 %broadcast_in_dim.2 = f32[64,1,128]{2,1,0:T(1,128)} broadcast(f32[128]{0:T(128)S(1)} %pad.4), dimensions={2} | broadcast | bytes 33280 | tf_op jit(solution)/shard_map/broadcast_in_dim | solution.py:251
  19.7 0.0 copy-start
  19.7 22.8 %all-to-all-start.1 = ((f32[64,1,128]{2,1,0:T(1,128)}), f32[64,1,128]{2,1,0:T(1,128)S(1)}, u32[]{:S(2)}, u32[]{:S(2)}) async-start(f32[64,1,128]{2,1,0:T(1,128)} %broadcast_in_dim.2), calls=%async_computation.1 | async-start | bytes 65536 | tf_op jit(solution)/shard_map/all_to_all | solution.py:253
  42.5 0.0 copy-done.1
  42.5 0.0 copy-done
  42.5 0.1 shard_map.156
  42.7 3.4 %collective-permute-start.2 = (f32[32,128]{1,0:T(8,128)S(1)}, f32[32,128]{1,0:T(8,128)S(1)}, u32[]{:S(2)}, u32[]{:S(2)}) collective-permute-start(f32[32,128]{1,0:T(8,128)S(1)} %get-tuple-element.24), channel_id=1, source_target_pairs={{0,1},{1,2},{2,3},{3,4},{4,5},{5,6},{6,7},{7,8},{8,9},{9,10},{10,1... | collective-permute-start | bytes 49160 | tf_op jit(solution)/shard_map/ppermute | solution.py:257
  46.1 5.8 %collective-permute-start.3 = (f32[32,128]{1,0:T(8,128)S(1)}, f32[32,128]{1,0:T(8,128)S(1)}, u32[]{:S(2)}, u32[]{:S(2)}) collective-permute-start(f32[32,128]{1,0:T(8,128)S(1)} %get-tuple-element.25), channel_id=1, source_target_pairs={{1,0},{2,1},{3,2},{4,3},{5,4},{6,5},{7,6},{8,7},{9,8},{10,9},{11,1... | collective-permute-start | bytes 49160 | tf_op jit(solution)/shard_map/ppermute | solution.py:258
  51.9 0.0 collective-permute-done.2.west_ref
  51.9 1.4 %collective-permute-done.3.east_ref = f32[32,128]{1,0:T(8,128)S(1)} collective-permute-done((f32[32,128]{1,0:T(8,128)S(1)}, f32[32,128]{1,0:T(8,128)S(1)}, u32[]{:S(2)}, u32[]{:S(2)}) %collective-permute-start.3) | collective-permute-done | bytes 16416 | tf_op jit(solution)/shard_map/ppermute | solution.py:258
  53.3 1.3 %shard_map.157 = (f32[2,16,128]{2,1,0:T(8,128)}, f32[3,16,128]{2,1,0:T(8,128)}) custom-call(f32[10,8,128]{2,1,0:T(8,128)S(1)} %copy-done, f32[10,8,128]{2,1,0:T(8,128)S(1)} %copy-done.1, f32[10,8,128]{2,1,0:T(8,128)S(1)} %collective-permute-done.before_ref, f32[10,8,128]{2,1,0:T(8,128)S(1)} %collective-permute-done.1.after_ref, ...), custom_call_target="tpu_custom_call" | custom-call | flops 2000000 | bytes 250000 | tf_op jit(solution)/shard_map/pallas_call | solution.py:204
  54.5 0.0 all-to-all-done.1
  54.5 0.6 %slice_reduce_fusion = f32[4]{0:T(128)} fusion(f32[64,1,128]{2,1,0:T(1,128)S(1)} %all-to-all-done.1), kind=kLoop, calls=%fused_computation | loop fusion | flops 252 | bytes 1040 | tf_op jit(solution)/shard_map/reduce_sum | solution.py:262
  (2 shorter events, 0.0 us)
Async XLA Ops:
  2.8 11.6 %all-to-all-start = ((f32[16,1,8]{2,1,0:T(1,128)}), f32[16,1,8]{2,1,0:T(1,128)S(1)}, u32[]{:S(2)}, u32[]{:S(2)}) async-start(f32[16,1,8]{2,1,0:T(1,128)} %get-tuple-element.21), calls=%async_computation | async-start | bytes 16384 | tf_op jit(solution)/shard_map/all_to_all | solution.py:244
  10.1 4.5 %collective-permute-start.1 = (f32[10,8,128]{2,1,0:T(8,128)}, f32[10,8,128]{2,1,0:T(8,128)S(1)}, u32[]{:S(2)}, u32[]{:S(2)}) collective-permute-start(f32[10,8,128]{2,1,0:T(8,128)} %get-tuple-element.19.first_ref), channel_id=1, source_target_pairs={{64,0},{128,64},{192,128},{256,192},{320,256},{384,320},{448,384},... | collective-permute-start | bytes 122888 | tf_op jit(solution)/shard_map/ppermute | solution.py:246
  12.3 6.7 %collective-permute-start = (f32[10,8,128]{2,1,0:T(8,128)}, f32[10,8,128]{2,1,0:T(8,128)S(1)}, u32[]{:S(2)}, u32[]{:S(2)}) collective-permute-start(f32[10,8,128]{2,1,0:T(8,128)} %get-tuple-element.20.last_ref), channel_id=1, source_target_pairs={{0,64},{64,128},{128,192},{192,256},{256,320},{320,384},{384,448},... | collective-permute-start | bytes 122888 | tf_op jit(solution)/shard_map/ppermute | solution.py:245
  19.0 23.5 %copy-start.1 = (f32[10,8,128]{2,1,0:T(8,128)S(1)}, f32[10,8,128]{2,1,0:T(8,128)}, u32[]{:S(2)}) copy-start(f32[10,8,128]{2,1,0:T(8,128)} %get-tuple-element.20.last_ref) | copy-start | bytes 122884
  19.7 22.9 %copy-start = (f32[10,8,128]{2,1,0:T(8,128)S(1)}, f32[10,8,128]{2,1,0:T(8,128)}, u32[]{:S(2)}) copy-start(f32[10,8,128]{2,1,0:T(8,128)} %get-tuple-element.19.first_ref) | copy-start | bytes 122884
  19.7 34.9 %all-to-all-start.1 = ((f32[64,1,128]{2,1,0:T(1,128)}), f32[64,1,128]{2,1,0:T(1,128)S(1)}, u32[]{:S(2)}, u32[]{:S(2)}) async-start(f32[64,1,128]{2,1,0:T(1,128)} %broadcast_in_dim.2), calls=%async_computation.1 | async-start | bytes 65536 | tf_op jit(solution)/shard_map/all_to_all | solution.py:253
  42.7 9.2 %collective-permute-start.2 = (f32[32,128]{1,0:T(8,128)S(1)}, f32[32,128]{1,0:T(8,128)S(1)}, u32[]{:S(2)}, u32[]{:S(2)}) collective-permute-start(f32[32,128]{1,0:T(8,128)S(1)} %get-tuple-element.24), channel_id=1, source_target_pairs={{0,1},{1,2},{2,3},{3,4},{4,5},{5,6},{6,7},{7,8},{8,9},{9,10},{10,1... | collective-permute-start | bytes 49160 | tf_op jit(solution)/shard_map/ppermute | solution.py:257
  46.1 7.2 %collective-permute-start.3 = (f32[32,128]{1,0:T(8,128)S(1)}, f32[32,128]{1,0:T(8,128)S(1)}, u32[]{:S(2)}, u32[]{:S(2)}) collective-permute-start(f32[32,128]{1,0:T(8,128)S(1)} %get-tuple-element.25), channel_id=1, source_target_pairs={{1,0},{2,1},{3,2},{4,3},{5,4},{6,5},{7,6},{8,7},{9,8},{10,9},{11,1... | collective-permute-start | bytes 49160 | tf_op jit(solution)/shard_map/ppermute | solution.py:258

commit v3 on v2

--- a/solution.py
+++ b/solution.py
@@ -22,6 +22,7 @@
 EDGE = 8
 WIDTH = 6
 THIRD = 1.0 / 1.5
+SLOT = 64
 
 
 def columns_step(temp, depth, surf):
@@ -157,9 +158,13 @@
 
 
 def subcycles_kernel(
-    first_ref, last_ref, before_ref, after_ref, west_ref, east_ref, velocity_out, stress_out
+    first_ref, last_ref, before_ref, after_ref, west_ref, east_ref, shares_ref, velocity_out, stress_out,
+    zonal_out,
 ):
     rows, cols = velocity_out.shape[1:]
+    zonal = jnp.sum(shares_ref[...], axis=0)
+    for j in range(BANDS_DEV):
+        zonal_out[j] = jnp.sum(jnp.where(lanes_of(zonal.shape) == j, zonal, 0.0))
     west, onward = west_ref[...], east_ref[...]
     lanes = lanes_of(west.shape)
     fields = []
@@ -194,10 +199,12 @@
     stress_out[2] = s12[:rows, :cols]
 
 
-def call(kernel, outs, flops, fetch=False):
+def call(kernel, outs, flops, fetch=False, smem_out=False):
     def run(*args):
         space = pltpu.HBM if fetch else pltpu.VMEM
-        scratch = []
+        scratch, spaces = [], [pltpu.VMEM] * len(outs)
+        if smem_out:
+            spaces[-1] = pltpu.SMEM
         if fetch:
             scratch = [pltpu.VMEM(a.shape, a.dtype) for a in args[:-1]]
             scratch += [pltpu.SMEM(args[-1].shape, jnp.int32), pltpu.SemaphoreType.DMA((len(args),))]
@@ -205,7 +212,7 @@
             kernel,
             out_shape=[jax.ShapeDtypeStruct(shape, jnp.float32) for shape in outs],
             in_specs=[pl.BlockSpec(memory_space=space)] * len(args),
-            out_specs=[pl.BlockSpec(memory_space=pltpu.VMEM)] * len(outs),
+            out_specs=[pl.BlockSpec(memory_space=where) for where in spaces],
             scratch_shapes=scratch,
             compiler_params=pltpu.CompilerParams(vmem_limit_bytes=(60 if fetch else 8) << 20),
             cost_estimate=pl.CostEstimate(flops=flops, bytes_accessed=flops // 8, transcendentals=0),
@@ -247,19 +254,17 @@
 
     total = jnp.sum(arrived, axis=(0, 1))
     share = total[:BANDS_DEV] / (total[BANDS_DEV:] * float(cols * lon_size))
-    share = jnp.pad(share, (0, cols - BANDS_DEV))
-    spread = jnp.broadcast_to(share[None, None], (lon_size, 1, cols))
-    spread, before, after = lax.optimization_barrier((spread, before, after))
+    share = jnp.pad(share, (0, SLOT - BANDS_DEV))
+    spread = jnp.broadcast_to(share[None, None], (lon_size, 1, SLOT))
     shares = lax.all_to_all(spread, "lon", 0, 0, tiled=True)
 
     packed = (4 * EDGE, cols)
-    right, left = call(pack_kernel, [packed, packed], 500_000)(first, last, before, after)
+    right, left = call(pack_kernel, [packed, packed], 500000)(first, last, before, after)
     west = lax.ppermute(right, "lon", [(i, (i + 1) % lon_size) for i in range(lon_size)])
     onward = lax.ppermute(left, "lon", [((i + 1) % lon_size, i) for i in range(lon_size)])
-    moving, stresses = call(
-        subcycles_kernel, [(2, rows, cols), (3, rows, cols)], 2_000_000
-    )(first, last, before, after, west, onward)
-    zonal_volume = jnp.sum(shares[:, :, :BANDS_DEV], axis=(0, 1))
+    moving, stresses, zonal_volume = call(
+        subcycles_kernel, [(2, rows, cols), (3, rows, cols), (BANDS_DEV,)], 2000000, smem_out=True
+    )(first, last, before, after, west, onward, shares)
     return (swap(temp_after), swap(thick_after), moving, stresses, zonal_volume)
 
 

time: 55.5 us -> 54.6 us (0.984)
  the two profiles are of different devices: /device:TPU:72 before, /device:TPU:1 now
where the time goes in v3:
time: 54.6 us; the launch traced here: 54.2 us
  starting transfers between devices  45.7 us (84%)
  Pallas kernels  3.61 us (7%)
  waiting for transfers between devices  3.44 us (6%)
  between operations  0.73 us (1%)
  local copies, waits for them, and re-layouts  0.64 us (1%)
    all_to_all x1, starting transfers between devices, local(): arrived = lax.all_to_all(parts, 'lat', 0, 0, tiled=True)  17.4 us
    all_to_all x1, starting transfers between devices, local(): shares = lax.all_to_all(spread, 'lon', 0, 0, tiled=True)  14.1 us
    ppermute x1, starting transfers between devices, local(): lax.ppermute(left, 'lon', [((i + 1) % lon_size, i) for i in range(lon_siz...  5.68 us
    pallas_call x3, Pallas kernels, run(): pl.pallas_call(kernel, out_shape=[jax.ShapeDtypeStruct(shape, jnp.float32...  3.61 us
    ppermute x1, starting transfers between devices, local(): lax.ppermute(last, 'lat', [(i, i + 1) for i in range(lat_size - 1)])  3.42 us
    ppermute x1, starting transfers between devices, local(): lax.ppermute(right, 'lon', [(i, (i + 1) % lon_size) for i in range(lon_si...  2.92 us
    ppermute x1, starting transfers between devices, local(): lax.ppermute(first, 'lat', [(i + 1, i) for i in range(lat_size - 1)])  2.13 us
    all_to_all x1, waiting for transfers between devices, local(): shares = lax.all_to_all(spread, 'lon', 0, 0, tiled=True)  2.01 us
  transfers between devices with their start and end apart: 6, of which 2 were waited for; matrix products, arithmetic and copies ran while one was open for 1% of the time, Pallas kernels for 0%

profile of v3, /device:TPU:1, one launch (start us, length us, event | category | flops | bytes accessed | tf_op | source)
XLA Modules:
  0.0 54.2 jit_solution(12681623019224828006)
XLA Ops:
  0.6 2.2 %shard_map.155 = (f32[35,16,128]{2,1,0:T(8,128)}, f32[5,16,128]{2,1,0:T(8,128)}, f32[16,1,8]{2,1,0:T(1,128)}, f32[10,8,128]{2,1,0:T(8,128)}, f32[10,8,128]{2,1,0:T(8,128)}) custom-call(f32[35,16,128]{2,1,0:T(8,128)} %bitcast.5, f32[5,16,128]{2,1,0:T(8,128)} %bitcast.6, f32[5,16,128]{2,1,0:T(8,128)} %bitcast.7, f32[16,128]{1,0:T(8,128)} %refs_3_.1, ...), custom_call_target="tpu_custom_call" | custom-call | flops 4000000 | bytes 500000 | tf_op jit(solution)/shard_map/pallas_call | solution.py:211
  2.8 17.4 %all-to-all-start = ((f32[16,1,8]{2,1,0:T(1,128)}), f32[16,1,8]{2,1,0:T(1,128)S(1)}, u32[]{:S(2)}, u32[]{:S(2)}) async-start(f32[16,1,8]{2,1,0:T(1,128)} %get-tuple-element.21), calls=%async_computation | async-start | bytes 16384 | tf_op jit(solution)/shard_map/all_to_all | solution.py:251
  20.3 2.1 %collective-permute-start.1 = (f32[10,8,128]{2,1,0:T(8,128)}, f32[10,8,128]{2,1,0:T(8,128)S(1)}, u32[]{:S(2)}, u32[]{:S(2)}) collective-permute-start(f32[10,8,128]{2,1,0:T(8,128)} %get-tuple-element.17.first_ref), channel_id=1, source_target_pairs={{64,0},{128,64},{192,128},{256,192},{320,256},{384,320},{448,384},... | collective-permute-start | bytes 122888 | tf_op jit(solution)/shard_map/ppermute | solution.py:253
  22.4 3.4 %collective-permute-start = (f32[10,8,128]{2,1,0:T(8,128)}, f32[10,8,128]{2,1,0:T(8,128)S(1)}, u32[]{:S(2)}, u32[]{:S(2)}) collective-permute-start(f32[10,8,128]{2,1,0:T(8,128)} %get-tuple-element.18.last_ref), channel_id=1, source_target_pairs={{0,64},{64,128},{128,192},{192,256},{256,320},{320,384},{384,448},... | collective-permute-start | bytes 122888 | tf_op jit(solution)/shard_map/ppermute | solution.py:252
  25.8 1.4 %all-to-all-done = f32[16,1,8]{2,1,0:T(1,128)S(1)} async-done(((f32[16,1,8]{2,1,0:T(1,128)}), f32[16,1,8]{2,1,0:T(1,128)S(1)}, u32[]{:S(2)}, u32[]{:S(2)}) %all-to-all-start) | async-done | bytes 544 | tf_op jit(solution)/shard_map/all_to_all | solution.py:251
  27.3 0.1 multiply_divide_fusion
  27.4 0.0 copy-start.1
  27.4 0.6 %broadcast_in_dim.2 = f32[64,1,64]{2,1,0:T(1,128)} broadcast(f32[64]{0:T(128)S(1)} %pad.4), dimensions={2} | broadcast | bytes 16640 | tf_op jit(solution)/shard_map/broadcast_in_dim | solution.py:258
  28.0 0.0 copy-start
  28.0 14.1 %all-to-all-start.1 = ((f32[64,1,64]{2,1,0:T(1,128)}), f32[64,1,64]{2,1,0:T(1,128)S(1)}, u32[]{:S(2)}, u32[]{:S(2)}) async-start(f32[64,1,64]{2,1,0:T(1,128)} %broadcast_in_dim.2), calls=%async_computation.1 | async-start | bytes 65536 | tf_op jit(solution)/shard_map/all_to_all | solution.py:259
  42.1 0.0 collective-permute-done.1.after_ref
  42.1 0.0 collective-permute-done.before_ref
  42.1 0.0 copy-done.1
  42.1 0.0 copy-done
  42.1 0.1 shard_map.156
  42.3 2.9 %collective-permute-start.2 = (f32[32,128]{1,0:T(8,128)S(1)}, f32[32,128]{1,0:T(8,128)S(1)}, u32[]{:S(2)}, u32[]{:S(2)}) collective-permute-start(f32[32,128]{1,0:T(8,128)S(1)} %get-tuple-element.19), channel_id=1, source_target_pairs={{0,1},{1,2},{2,3},{3,4},{4,5},{5,6},{6,7},{7,8},{8,9},{9,10},{10,1... | collective-permute-start | bytes 49160 | tf_op jit(solution)/shard_map/ppermute | solution.py:263
  45.2 5.7 %collective-permute-start.3 = (f32[32,128]{1,0:T(8,128)S(1)}, f32[32,128]{1,0:T(8,128)S(1)}, u32[]{:S(2)}, u32[]{:S(2)}) collective-permute-start(f32[32,128]{1,0:T(8,128)S(1)} %get-tuple-element.20), channel_id=1, source_target_pairs={{1,0},{2,1},{3,2},{4,3},{5,4},{6,5},{7,6},{8,7},{9,8},{10,9},{11,1... | collective-permute-start | bytes 49160 | tf_op jit(solution)/shard_map/ppermute | solution.py:264
  50.9 2.0 %all-to-all-done.1.shares_ref = f32[64,1,64]{2,1,0:T(1,128)S(1)} async-done(((f32[64,1,64]{2,1,0:T(1,128)}), f32[64,1,64]{2,1,0:T(1,128)S(1)}, u32[]{:S(2)}, u32[]{:S(2)}) %all-to-all-start.1) | async-done | bytes 16416 | tf_op jit(solution)/shard_map/all_to_all | solution.py:259
  52.9 0.0 collective-permute-done.2.west_ref
  52.9 0.0 collective-permute-done.3.east_ref
  52.9 1.3 %shard_map.157 = (f32[2,16,128]{2,1,0:T(8,128)}, f32[3,16,128]{2,1,0:T(8,128)}, f32[4]{0:T(128)}) custom-call(f32[10,8,128]{2,1,0:T(8,128)S(1)} %copy-done, f32[10,8,128]{2,1,0:T(8,128)S(1)} %copy-done.1, f32[10,8,128]{2,1,0:T(8,128)S(1)} %collective-permute-done.before_ref, f32[10,8,128]{2,1,0:T(8,128)S(1)} %collective-permute-done.1.after_ref, ...), custom_call_target="tpu_custom_call" | custom-call | flops 2000000 | bytes 250000 | tf_op jit(solution)/shard_map/pallas_call | solution.py:211
  (2 shorter events, 0.0 us)
Async XLA Ops:
  2.8 24.4 %all-to-all-start = ((f32[16,1,8]{2,1,0:T(1,128)}), f32[16,1,8]{2,1,0:T(1,128)S(1)}, u32[]{:S(2)}, u32[]{:S(2)}) async-start(f32[16,1,8]{2,1,0:T(1,128)} %get-tuple-element.21), calls=%async_computation | async-start | bytes 16384 | tf_op jit(solution)/shard_map/all_to_all | solution.py:251
  20.3 21.8 %collective-permute-start.1 = (f32[10,8,128]{2,1,0:T(8,128)}, f32[10,8,128]{2,1,0:T(8,128)S(1)}, u32[]{:S(2)}, u32[]{:S(2)}) collective-permute-start(f32[10,8,128]{2,1,0:T(8,128)} %get-tuple-element.17.first_ref), channel_id=1, source_target_pairs={{64,0},{128,64},{192,128},{256,192},{320,256},{384,320},{448,384},... | collective-permute-start | bytes 122888 | tf_op jit(solution)/shard_map/ppermute | solution.py:253
  22.4 19.7 %collective-permute-start = (f32[10,8,128]{2,1,0:T(8,128)}, f32[10,8,128]{2,1,0:T(8,128)S(1)}, u32[]{:S(2)}, u32[]{:S(2)}) collective-permute-start(f32[10,8,128]{2,1,0:T(8,128)} %get-tuple-element.18.last_ref), channel_id=1, source_target_pairs={{0,64},{64,128},{128,192},{192,256},{256,320},{320,384},{384,448},... | collective-permute-start | bytes 122888 | tf_op jit(solution)/shard_map/ppermute | solution.py:252
  27.4 14.7 %copy-start.1 = (f32[10,8,128]{2,1,0:T(8,128)S(1)}, f32[10,8,128]{2,1,0:T(8,128)}, u32[]{:S(2)}) copy-start(f32[10,8,128]{2,1,0:T(8,128)} %get-tuple-element.18.last_ref) | copy-start | bytes 122884
  28.0 14.1 %copy-start = (f32[10,8,128]{2,1,0:T(8,128)S(1)}, f32[10,8,128]{2,1,0:T(8,128)}, u32[]{:S(2)}) copy-start(f32[10,8,128]{2,1,0:T(8,128)} %get-tuple-element.17.first_ref) | copy-start | bytes 122884
  28.0 24.9 %all-to-all-start.1 = ((f32[64,1,64]{2,1,0:T(1,128)}), f32[64,1,64]{2,1,0:T(1,128)S(1)}, u32[]{:S(2)}, u32[]{:S(2)}) async-start(f32[64,1,64]{2,1,0:T(1,128)} %broadcast_in_dim.2), calls=%async_computation.1 | async-start | bytes 65536 | tf_op jit(solution)/shard_map/all_to_all | solution.py:259
  42.3 10.6 %collective-permute-start.2 = (f32[32,128]{1,0:T(8,128)S(1)}, f32[32,128]{1,0:T(8,128)S(1)}, u32[]{:S(2)}, u32[]{:S(2)}) collective-permute-start(f32[32,128]{1,0:T(8,128)S(1)} %get-tuple-element.19), channel_id=1, source_target_pairs={{0,1},{1,2},{2,3},{3,4},{4,5},{5,6},{6,7},{7,8},{8,9},{9,10},{10,1... | collective-permute-start | bytes 49160 | tf_op jit(solution)/shard_map/ppermute | solution.py:263
  45.2 7.7 %collective-permute-start.3 = (f32[32,128]{1,0:T(8,128)S(1)}, f32[32,128]{1,0:T(8,128)S(1)}, u32[]{:S(2)}, u32[]{:S(2)}) collective-permute-start(f32[32,128]{1,0:T(8,128)S(1)} %get-tuple-element.20), channel_id=1, source_target_pairs={{1,0},{2,1},{3,2},{4,3},{5,4},{6,5},{7,6},{8,7},{9,8},{10,9},{11,1... | collective-permute-start | bytes 49160 | tf_op jit(solution)/shard_map/ppermute | solution.py:264

commit v4 on v2

--- a/solution.py
+++ b/solution.py
@@ -22,6 +22,7 @@
 EDGE = 8
 WIDTH = 6
 THIRD = 1.0 / 1.5
+SLOT = 128
 
 
 def columns_step(temp, depth, surf):
@@ -247,13 +248,12 @@
 
     total = jnp.sum(arrived, axis=(0, 1))
     share = total[:BANDS_DEV] / (total[BANDS_DEV:] * float(cols * lon_size))
-    share = jnp.pad(share, (0, cols - BANDS_DEV))
-    spread = jnp.broadcast_to(share[None, None], (lon_size, 1, cols))
-    spread, before, after = lax.optimization_barrier((spread, before, after))
+    share = jnp.pad(share, (0, SLOT - BANDS_DEV))
+    spread = jnp.broadcast_to(share[None, None], (lon_size, 1, SLOT))
     shares = lax.all_to_all(spread, "lon", 0, 0, tiled=True)
 
     packed = (4 * EDGE, cols)
-    right, left = call(pack_kernel, [packed, packed], 500_000)(first, last, before, after)
+    right, left = call(pack_kernel, [packed, packed], 200_000_000)(first, last, before, after)
     west = lax.ppermute(right, "lon", [(i, (i + 1) % lon_size) for i in range(lon_size)])
     onward = lax.ppermute(left, "lon", [((i + 1) % lon_size, i) for i in range(lon_size)])
     moving, stresses = call(

time: 55.5 us -> 54.6 us (0.984)
  the two profiles are of different devices: /device:TPU:72 before, /device:TPU:1 now
where the time goes in v4:
time: 54.6 us; the launch traced here: 53.6 us
  starting transfers between devices  45.7 us (84%)
  Pallas kernels  3.6 us (7%)
  waiting for transfers between devices  2.26 us (4%)
  between operations  0.74 us (1%)
  other arithmetic  0.71 us (1%)
  local copies, waits for them, and re-layouts  0.64 us (1%)
    all_to_all x1, starting transfers between devices, local(): arrived = lax.all_to_all(parts, 'lat', 0, 0, tiled=True)  17.4 us
    all_to_all x1, starting transfers between devices, local(): shares = lax.all_to_all(spread, 'lon', 0, 0, tiled=True)  14.1 us
    ppermute x1, starting transfers between devices, local(): lax.ppermute(left, 'lon', [((i + 1) % lon_size, i) for i in range(lon_siz...  5.68 us
    pallas_call x3, Pallas kernels, run(): pl.pallas_call(kernel, out_shape=[jax.ShapeDtypeStruct(shape, jnp.float32...  3.6 us
    ppermute x1, starting transfers between devices, local(): lax.ppermute(last, 'lat', [(i, i + 1) for i in range(lat_size - 1)])  3.42 us
    ppermute x1, starting transfers between devices, local(): lax.ppermute(right, 'lon', [(i, (i + 1) % lon_size) for i in range(lon_si...  2.92 us
    ppermute x1, starting transfers between devices, local(): lax.ppermute(first, 'lat', [(i + 1, i) for i in range(lat_size - 1)])  2.13 us
    all_to_all x1, waiting for transfers between devices, local(): arrived = lax.all_to_all(parts, 'lat', 0, 0, tiled=True)  1.42 us
  transfers between devices with their start and end apart: 6, of which 2 were waited for; matrix products, arithmetic and copies ran while one was open for 1% of the time, Pallas kernels for 3%

profile of v4, /device:TPU:1, one launch (start us, length us, event | category | flops | bytes accessed | tf_op | source)
XLA Modules:
  0.0 53.6 jit_solution(9906304090432923909)
XLA Ops:
  0.6 2.2 %shard_map.155 = (f32[35,16,128]{2,1,0:T(8,128)}, f32[5,16,128]{2,1,0:T(8,128)}, f32[16,1,8]{2,1,0:T(1,128)}, f32[10,8,128]{2,1,0:T(8,128)}, f32[10,8,128]{2,1,0:T(8,128)}) custom-call(f32[35,16,128]{2,1,0:T(8,128)} %bitcast.5, f32[5,16,128]{2,1,0:T(8,128)} %bitcast.6, f32[5,16,128]{2,1,0:T(8,128)} %bitcast.7, f32[16,128]{1,0:T(8,128)} %refs_3_.1, ...), custom_call_target="tpu_custom_call" | custom-call | flops 4000000 | bytes 500000 | tf_op jit(solution)/shard_map/pallas_call | solution.py:205
  2.8 17.4 %all-to-all-start = ((f32[16,1,8]{2,1,0:T(1,128)}), f32[16,1,8]{2,1,0:T(1,128)S(1)}, u32[]{:S(2)}, u32[]{:S(2)}) async-start(f32[16,1,8]{2,1,0:T(1,128)} %get-tuple-element.22), calls=%async_computation | async-start | bytes 16384 | tf_op jit(solution)/shard_map/all_to_all | solution.py:245
  20.3 2.1 %collective-permute-start.1 = (f32[10,8,128]{2,1,0:T(8,128)}, f32[10,8,128]{2,1,0:T(8,128)S(1)}, u32[]{:S(2)}, u32[]{:S(2)}) collective-permute-start(f32[10,8,128]{2,1,0:T(8,128)} %get-tuple-element.16.first_ref), channel_id=1, source_target_pairs={{64,0},{128,64},{192,128},{256,192},{320,256},{384,320},{448,384},... | collective-permute-start | bytes 122888 | tf_op jit(solution)/shard_map/ppermute | solution.py:247
  22.4 3.4 %collective-permute-start = (f32[10,8,128]{2,1,0:T(8,128)}, f32[10,8,128]{2,1,0:T(8,128)S(1)}, u32[]{:S(2)}, u32[]{:S(2)}) collective-permute-start(f32[10,8,128]{2,1,0:T(8,128)} %get-tuple-element.17.last_ref), channel_id=1, source_target_pairs={{0,64},{64,128},{128,192},{192,256},{256,320},{320,384},{384,448},... | collective-permute-start | bytes 122888 | tf_op jit(solution)/shard_map/ppermute | solution.py:246
  25.8 1.4 %all-to-all-done = f32[16,1,8]{2,1,0:T(1,128)S(1)} async-done(((f32[16,1,8]{2,1,0:T(1,128)}), f32[16,1,8]{2,1,0:T(1,128)S(1)}, u32[]{:S(2)}, u32[]{:S(2)}) %all-to-all-start) | async-done | bytes 544 | tf_op jit(solution)/shard_map/all_to_all | solution.py:245
  27.3 0.1 multiply_divide_fusion
  27.4 0.0 copy-start.1
  27.4 0.6 %broadcast_in_dim.2 = f32[64,1,128]{2,1,0:T(1,128)} broadcast(f32[128]{0:T(128)S(1)} %pad.4), dimensions={2} | broadcast | bytes 33280 | tf_op jit(solution)/shard_map/broadcast_in_dim | solution.py:252
  28.0 0.0 copy-start
  28.0 14.1 %all-to-all-start.1 = ((f32[64,1,128]{2,1,0:T(1,128)}), f32[64,1,128]{2,1,0:T(1,128)S(1)}, u32[]{:S(2)}, u32[]{:S(2)}) async-start(f32[64,1,128]{2,1,0:T(1,128)} %broadcast_in_dim.2), calls=%async_computation.1 | async-start | bytes 65536 | tf_op jit(solution)/shard_map/all_to_all | solution.py:253
  42.1 0.0 collective-permute-done.1.after_ref
  42.1 0.0 collective-permute-done.before_ref
  42.1 0.0 copy-done.1
  42.1 0.0 copy-done
  42.1 0.1 shard_map.156
  42.3 2.9 %collective-permute-start.2 = (f32[32,128]{1,0:T(8,128)S(1)}, f32[32,128]{1,0:T(8,128)S(1)}, u32[]{:S(2)}, u32[]{:S(2)}) collective-permute-start(f32[32,128]{1,0:T(8,128)S(1)} %get-tuple-element.18), channel_id=1, source_target_pairs={{0,1},{1,2},{2,3},{3,4},{4,5},{5,6},{6,7},{7,8},{8,9},{9,10},{10,1... | collective-permute-start | bytes 49160 | tf_op jit(solution)/shard_map/ppermute | solution.py:257
  45.2 5.7 %collective-permute-start.3 = (f32[32,128]{1,0:T(8,128)S(1)}, f32[32,128]{1,0:T(8,128)S(1)}, u32[]{:S(2)}, u32[]{:S(2)}) collective-permute-start(f32[32,128]{1,0:T(8,128)S(1)} %get-tuple-element.19), channel_id=1, source_target_pairs={{1,0},{2,1},{3,2},{4,3},{5,4},{6,5},{7,6},{8,7},{9,8},{10,9},{11,1... | collective-permute-start | bytes 49160 | tf_op jit(solution)/shard_map/ppermute | solution.py:258
  50.9 0.0 collective-permute-done.2.west_ref
  50.9 0.8 %collective-permute-done.3.east_ref = f32[32,128]{1,0:T(8,128)S(1)} collective-permute-done((f32[32,128]{1,0:T(8,128)S(1)}, f32[32,128]{1,0:T(8,128)S(1)}, u32[]{:S(2)}, u32[]{:S(2)}) %collective-permute-start.3) | collective-permute-done | bytes 16416 | tf_op jit(solution)/shard_map/ppermute | solution.py:258
  51.8 1.3 %shard_map.157 = (f32[2,16,128]{2,1,0:T(8,128)}, f32[3,16,128]{2,1,0:T(8,128)}) custom-call(f32[10,8,128]{2,1,0:T(8,128)S(1)} %copy-done, f32[10,8,128]{2,1,0:T(8,128)S(1)} %copy-done.1, f32[10,8,128]{2,1,0:T(8,128)S(1)} %collective-permute-done.before_ref, f32[10,8,128]{2,1,0:T(8,128)S(1)} %collective-permute-done.1.after_ref, ...), custom_call_target="tpu_custom_call" | custom-call | flops 2000000 | bytes 250000 | tf_op jit(solution)/shard_map/pallas_call | solution.py:205
  53.0 0.0 all-to-all-done.1
  53.0 0.6 %slice_reduce_fusion = f32[4]{0:T(128)} fusion(f32[64,1,128]{2,1,0:T(1,128)S(1)} %all-to-all-done.1), kind=kLoop, calls=%fused_computation | loop fusion | flops 252 | bytes 1040 | tf_op jit(solution)/shard_map/reduce_sum | solution.py:262
  (2 shorter events, 0.0 us)
Async XLA Ops:
  2.8 24.4 %all-to-all-start = ((f32[16,1,8]{2,1,0:T(1,128)}), f32[16,1,8]{2,1,0:T(1,128)S(1)}, u32[]{:S(2)}, u32[]{:S(2)}) async-start(f32[16,1,8]{2,1,0:T(1,128)} %get-tuple-element.22), calls=%async_computation | async-start | bytes 16384 | tf_op jit(solution)/shard_map/all_to_all | solution.py:245
  20.3 21.8 %collective-permute-start.1 = (f32[10,8,128]{2,1,0:T(8,128)}, f32[10,8,128]{2,1,0:T(8,128)S(1)}, u32[]{:S(2)}, u32[]{:S(2)}) collective-permute-start(f32[10,8,128]{2,1,0:T(8,128)} %get-tuple-element.16.first_ref), channel_id=1, source_target_pairs={{64,0},{128,64},{192,128},{256,192},{320,256},{384,320},{448,384},... | collective-permute-start | bytes 122888 | tf_op jit(solution)/shard_map/ppermute | solution.py:247
  22.4 19.7 %collective-permute-start = (f32[10,8,128]{2,1,0:T(8,128)}, f32[10,8,128]{2,1,0:T(8,128)S(1)}, u32[]{:S(2)}, u32[]{:S(2)}) collective-permute-start(f32[10,8,128]{2,1,0:T(8,128)} %get-tuple-element.17.last_ref), channel_id=1, source_target_pairs={{0,64},{64,128},{128,192},{192,256},{256,320},{320,384},{384,448},... | collective-permute-start | bytes 122888 | tf_op jit(solution)/shard_map/ppermute | solution.py:246
  27.4 14.7 %copy-start.1 = (f32[10,8,128]{2,1,0:T(8,128)S(1)}, f32[10,8,128]{2,1,0:T(8,128)}, u32[]{:S(2)}) copy-start(f32[10,8,128]{2,1,0:T(8,128)} %get-tuple-element.17.last_ref) | copy-start | bytes 122884
  28.0 14.1 %copy-start = (f32[10,8,128]{2,1,0:T(8,128)S(1)}, f32[10,8,128]{2,1,0:T(8,128)}, u32[]{:S(2)}) copy-start(f32[10,8,128]{2,1,0:T(8,128)} %get-tuple-element.16.first_ref) | copy-start | bytes 122884
  28.0 25.0 %all-to-all-start.1 = ((f32[64,1,128]{2,1,0:T(1,128)}), f32[64,1,128]{2,1,0:T(1,128)S(1)}, u32[]{:S(2)}, u32[]{:S(2)}) async-start(f32[64,1,128]{2,1,0:T(1,128)} %broadcast_in_dim.2), calls=%async_computation.1 | async-start | bytes 65536 | tf_op jit(solution)/shard_map/all_to_all | solution.py:253
  42.3 8.6 %collective-permute-start.2 = (f32[32,128]{1,0:T(8,128)S(1)}, f32[32,128]{1,0:T(8,128)S(1)}, u32[]{:S(2)}, u32[]{:S(2)}) collective-permute-start(f32[32,128]{1,0:T(8,128)S(1)} %get-tuple-element.18), channel_id=1, source_target_pairs={{0,1},{1,2},{2,3},{3,4},{4,5},{5,6},{6,7},{7,8},{8,9},{9,10},{10,1... | collective-permute-start | bytes 49160 | tf_op jit(solution)/shard_map/ppermute | solution.py:257
  45.2 6.5 %collective-permute-start.3 = (f32[32,128]{1,0:T(8,128)S(1)}, f32[32,128]{1,0:T(8,128)S(1)}, u32[]{:S(2)}, u32[]{:S(2)}) collective-permute-start(f32[32,128]{1,0:T(8,128)S(1)} %get-tuple-element.19), channel_id=1, source_target_pairs={{1,0},{2,1},{3,2},{4,3},{5,4},{6,5},{7,6},{8,7},{9,8},{10,9},{11,1... | collective-permute-start | bytes 49160 | tf_op jit(solution)/shard_map/ppermute | solution.py:258

commit v5 on v3

--- a/solution.py
+++ b/solution.py
@@ -69,7 +69,7 @@
 
 def columns_body(
     temp_ref, depth_ref, area_ref, surf_ref, sea_ref, velocity_ref, stress_ref, wind_ref, current_ref,
-    land_ref, ice_ref, band_ref, temp_out, thick_out, parts_out, first_out, last_out,
+    land_ref, ice_ref, band_ref, temp_out, thick_out, parts_out, last_out, first_out,
 ):
     rows = surf_ref.shape[0]
     depth, area = depth_ref[...], area_ref[...]
@@ -132,7 +132,7 @@
     return lax.broadcasted_iota(jnp.int32, shape, 1)
 
 
-def pack_kernel(first_ref, last_ref, before_ref, after_ref, right_out, left_out):
+def pack_kernel(last_ref, first_ref, before_ref, after_ref, right_out, left_out):
     cols = right_out.shape[1]
     lanes = lanes_of(right_out.shape)
     right = jnp.zeros(right_out.shape, jnp.float32)
@@ -158,7 +158,7 @@
 
 
 def subcycles_kernel(
-    first_ref, last_ref, before_ref, after_ref, west_ref, east_ref, shares_ref, velocity_out, stress_out,
+    last_ref, first_ref, before_ref, after_ref, west_ref, east_ref, shares_ref, velocity_out, stress_out,
     zonal_out,
 ):
     rows, cols = velocity_out.shape[1:]
@@ -239,7 +239,7 @@
     lat_size, lon_size = lax.axis_size("lat"), lax.axis_size("lon")
     half = (PLANES, EDGE, cols)
     swap = lambda x: jnp.transpose(x, (1, 0, 2))
-    temp_after, thick_after, parts, first, last = call(
+    temp_after, thick_after, parts, last, first = call(
         columns_kernel,
         [(levels, rows, cols), (DEPTH_CLASSES, rows, cols), (lat_size, 1, 2 * BANDS_DEV), half, half],
         4_000_000,
@@ -259,12 +259,12 @@
     shares = lax.all_to_all(spread, "lon", 0, 0, tiled=True)
 
     packed = (4 * EDGE, cols)
-    right, left = call(pack_kernel, [packed, packed], 500000)(first, last, before, after)
+    right, left = call(pack_kernel, [packed, packed], 500000)(last, first, before, after)
     west = lax.ppermute(right, "lon", [(i, (i + 1) % lon_size) for i in range(lon_size)])
     onward = lax.ppermute(left, "lon", [((i + 1) % lon_size, i) for i in range(lon_size)])
     moving, stresses, zonal_volume = call(
         subcycles_kernel, [(2, rows, cols), (3, rows, cols), (BANDS_DEV,)], 2000000, smem_out=True
-    )(first, last, before, after, west, onward, shares)
+    )(last, first, before, after, west, onward, shares)
     return (swap(temp_after), swap(thick_after), moving, stresses, zonal_volume)
 
 

time: 54.6 us -> 54.6 us (level)
  no operation moved by 1% of the time
where the time goes in v5:
time: 54.6 us; the launch traced here: 54.2 us
  starting transfers between devices  45.6 us (84%)
  Pallas kernels  3.61 us (7%)
  waiting for transfers between devices  3.53 us (6%)
  between operations  0.73 us (1%)
  local copies, waits for them, and re-layouts  0.64 us (1%)
    all_to_all x1, starting transfers between devices, local(): arrived = lax.all_to_all(parts, 'lat', 0, 0, tiled=True)  17.4 us
    all_to_all x1, starting transfers between devices, local(): shares = lax.all_to_all(spread, 'lon', 0, 0, tiled=True)  14.1 us
    ppermute x1, starting transfers between devices, local(): lax.ppermute(left, 'lon', [((i + 1) % lon_size, i) for i in range(lon_siz...  5.68 us
    pallas_call x3, Pallas kernels, run(): pl.pallas_call(kernel, out_shape=[jax.ShapeDtypeStruct(shape, jnp.float32...  3.61 us
    ppermute x1, starting transfers between devices, local(): lax.ppermute(last, 'lat', [(i, i + 1) for i in range(lat_size - 1)])  3.53 us
    ppermute x1, starting transfers between devices, local(): lax.ppermute(right, 'lon', [(i, (i + 1) % lon_size) for i in range(lon_si...  2.92 us
    all_to_all x1, waiting for transfers between devices, local(): shares = lax.all_to_all(spread, 'lon', 0, 0, tiled=True)  2.01 us
    ppermute x1, starting transfers between devices, local(): lax.ppermute(first, 'lat', [(i + 1, i) for i in range(lat_size - 1)])  1.92 us
  transfers between devices with their start and end apart: 6, of which 2 were waited for; matrix products, arithmetic and copies ran while one was open for 1% of the time, Pallas kernels for 0%

profile of v5, /device:TPU:1, one launch (start us, length us, event | category | flops | bytes accessed | tf_op | source)
XLA Modules:
  0.0 54.2 jit_solution(10594806344527910356)
XLA Ops:
  0.6 2.2 %shard_map.155 = (f32[35,16,128]{2,1,0:T(8,128)}, f32[5,16,128]{2,1,0:T(8,128)}, f32[16,1,8]{2,1,0:T(1,128)}, f32[10,8,128]{2,1,0:T(8,128)}, f32[10,8,128]{2,1,0:T(8,128)}) custom-call(f32[35,16,128]{2,1,0:T(8,128)} %bitcast.5, f32[5,16,128]{2,1,0:T(8,128)} %bitcast.6, f32[5,16,128]{2,1,0:T(8,128)} %bitcast.7, f32[16,128]{1,0:T(8,128)} %refs_3_.1, ...), custom_call_target="tpu_custom_call" | custom-call | flops 4000000 | bytes 500000 | tf_op jit(solution)/shard_map/pallas_call | solution.py:211
  2.8 17.4 %all-to-all-start = ((f32[16,1,8]{2,1,0:T(1,128)}), f32[16,1,8]{2,1,0:T(1,128)S(1)}, u32[]{:S(2)}, u32[]{:S(2)}) async-start(f32[16,1,8]{2,1,0:T(1,128)} %get-tuple-element.21), calls=%async_computation | async-start | bytes 16384 | tf_op jit(solution)/shard_map/all_to_all | solution.py:251
  20.3 3.5 %collective-permute-start = (f32[10,8,128]{2,1,0:T(8,128)}, f32[10,8,128]{2,1,0:T(8,128)S(1)}, u32[]{:S(2)}, u32[]{:S(2)}) collective-permute-start(f32[10,8,128]{2,1,0:T(8,128)} %get-tuple-element.17.last_ref), channel_id=1, source_target_pairs={{0,64},{64,128},{128,192},{192,256},{256,320},{320,384},{384,448},... | collective-permute-start | bytes 122888 | tf_op jit(solution)/shard_map/ppermute | solution.py:252
  23.8 1.9 %collective-permute-start.1 = (f32[10,8,128]{2,1,0:T(8,128)}, f32[10,8,128]{2,1,0:T(8,128)S(1)}, u32[]{:S(2)}, u32[]{:S(2)}) collective-permute-start(f32[10,8,128]{2,1,0:T(8,128)} %get-tuple-element.18.first_ref), channel_id=1, source_target_pairs={{64,0},{128,64},{192,128},{256,192},{320,256},{384,320},{448,384},... | collective-permute-start | bytes 122888 | tf_op jit(solution)/shard_map/ppermute | solution.py:253
  25.7 1.5 %all-to-all-done = f32[16,1,8]{2,1,0:T(1,128)S(1)} async-done(((f32[16,1,8]{2,1,0:T(1,128)}), f32[16,1,8]{2,1,0:T(1,128)S(1)}, u32[]{:S(2)}, u32[]{:S(2)}) %all-to-all-start) | async-done | bytes 544 | tf_op jit(solution)/shard_map/all_to_all | solution.py:251
  27.3 0.1 multiply_divide_fusion
  27.4 0.0 copy-start.1
  27.4 0.6 %broadcast_in_dim.2 = f32[64,1,64]{2,1,0:T(1,128)} broadcast(f32[64]{0:T(128)S(1)} %pad.4), dimensions={2} | broadcast | bytes 16640 | tf_op jit(solution)/shard_map/broadcast_in_dim | solution.py:258
  28.0 0.0 copy-start
  28.0 14.1 %all-to-all-start.1 = ((f32[64,1,64]{2,1,0:T(1,128)}), f32[64,1,64]{2,1,0:T(1,128)S(1)}, u32[]{:S(2)}, u32[]{:S(2)}) async-start(f32[64,1,64]{2,1,0:T(1,128)} %broadcast_in_dim.2), calls=%async_computation.1 | async-start | bytes 65536 | tf_op jit(solution)/shard_map/all_to_all | solution.py:259
  42.1 0.0 collective-permute-done.before_ref
  42.1 0.0 collective-permute-done.1.after_ref
  42.1 0.0 copy-done.1
  42.1 0.0 copy-done
  42.1 0.1 shard_map.156
  42.3 2.9 %collective-permute-start.2 = (f32[32,128]{1,0:T(8,128)S(1)}, f32[32,128]{1,0:T(8,128)S(1)}, u32[]{:S(2)}, u32[]{:S(2)}) collective-permute-start(f32[32,128]{1,0:T(8,128)S(1)} %get-tuple-element.19), channel_id=1, source_target_pairs={{0,1},{1,2},{2,3},{3,4},{4,5},{5,6},{6,7},{7,8},{8,9},{9,10},{10,1... | collective-permute-start | bytes 49160 | tf_op jit(solution)/shard_map/ppermute | solution.py:263
  45.2 5.7 %collective-permute-start.3 = (f32[32,128]{1,0:T(8,128)S(1)}, f32[32,128]{1,0:T(8,128)S(1)}, u32[]{:S(2)}, u32[]{:S(2)}) collective-permute-start(f32[32,128]{1,0:T(8,128)S(1)} %get-tuple-element.20), channel_id=1, source_target_pairs={{1,0},{2,1},{3,2},{4,3},{5,4},{6,5},{7,6},{8,7},{9,8},{10,9},{11,1... | collective-permute-start | bytes 49160 | tf_op jit(solution)/shard_map/ppermute | solution.py:264
  50.9 2.0 %all-to-all-done.1.shares_ref = f32[64,1,64]{2,1,0:T(1,128)S(1)} async-done(((f32[64,1,64]{2,1,0:T(1,128)}), f32[64,1,64]{2,1,0:T(1,128)S(1)}, u32[]{:S(2)}, u32[]{:S(2)}) %all-to-all-start.1) | async-done | bytes 16416 | tf_op jit(solution)/shard_map/all_to_all | solution.py:259
  52.9 0.0 collective-permute-done.2.west_ref
  52.9 0.0 collective-permute-done.3.east_ref
  52.9 1.3 %shard_map.157 = (f32[2,16,128]{2,1,0:T(8,128)}, f32[3,16,128]{2,1,0:T(8,128)}, f32[4]{0:T(128)}) custom-call(f32[10,8,128]{2,1,0:T(8,128)S(1)} %copy-done, f32[10,8,128]{2,1,0:T(8,128)S(1)} %copy-done.1, f32[10,8,128]{2,1,0:T(8,128)S(1)} %collective-permute-done.before_ref, f32[10,8,128]{2,1,0:T(8,128)S(1)} %collective-permute-done.1.after_ref, ...), custom_call_target="tpu_custom_call" | custom-call | flops 2000000 | bytes 250000 | tf_op jit(solution)/shard_map/pallas_call | solution.py:211
  (2 shorter events, 0.0 us)
Async XLA Ops:
  2.8 24.4 %all-to-all-start = ((f32[16,1,8]{2,1,0:T(1,128)}), f32[16,1,8]{2,1,0:T(1,128)S(1)}, u32[]{:S(2)}, u32[]{:S(2)}) async-start(f32[16,1,8]{2,1,0:T(1,128)} %get-tuple-element.21), calls=%async_computation | async-start | bytes 16384 | tf_op jit(solution)/shard_map/all_to_all | solution.py:251
  20.3 21.8 %collective-permute-start = (f32[10,8,128]{2,1,0:T(8,128)}, f32[10,8,128]{2,1,0:T(8,128)S(1)}, u32[]{:S(2)}, u32[]{:S(2)}) collective-permute-start(f32[10,8,128]{2,1,0:T(8,128)} %get-tuple-element.17.last_ref), channel_id=1, source_target_pairs={{0,64},{64,128},{128,192},{192,256},{256,320},{320,384},{384,448},... | collective-permute-start | bytes 122888 | tf_op jit(solution)/shard_map/ppermute | solution.py:252
  23.8 18.3 %collective-permute-start.1 = (f32[10,8,128]{2,1,0:T(8,128)}, f32[10,8,128]{2,1,0:T(8,128)S(1)}, u32[]{:S(2)}, u32[]{:S(2)}) collective-permute-start(f32[10,8,128]{2,1,0:T(8,128)} %get-tuple-element.18.first_ref), channel_id=1, source_target_pairs={{64,0},{128,64},{192,128},{256,192},{320,256},{384,320},{448,384},... | collective-permute-start | bytes 122888 | tf_op jit(solution)/shard_map/ppermute | solution.py:253
  27.4 14.7 %copy-start.1 = (f32[10,8,128]{2,1,0:T(8,128)S(1)}, f32[10,8,128]{2,1,0:T(8,128)}, u32[]{:S(2)}) copy-start(f32[10,8,128]{2,1,0:T(8,128)} %get-tuple-element.18.first_ref) | copy-start | bytes 122884
  28.0 14.1 %copy-start = (f32[10,8,128]{2,1,0:T(8,128)S(1)}, f32[10,8,128]{2,1,0:T(8,128)}, u32[]{:S(2)}) copy-start(f32[10,8,128]{2,1,0:T(8,128)} %get-tuple-element.17.last_ref) | copy-start | bytes 122884
  28.0 24.9 %all-to-all-start.1 = ((f32[64,1,64]{2,1,0:T(1,128)}), f32[64,1,64]{2,1,0:T(1,128)S(1)}, u32[]{:S(2)}, u32[]{:S(2)}) async-start(f32[64,1,64]{2,1,0:T(1,128)} %broadcast_in_dim.2), calls=%async_computation.1 | async-start | bytes 65536 | tf_op jit(solution)/shard_map/all_to_all | solution.py:259
  42.3 10.6 %collective-permute-start.2 = (f32[32,128]{1,0:T(8,128)S(1)}, f32[32,128]{1,0:T(8,128)S(1)}, u32[]{:S(2)}, u32[]{:S(2)}) collective-permute-start(f32[32,128]{1,0:T(8,128)S(1)} %get-tuple-element.19), channel_id=1, source_target_pairs={{0,1},{1,2},{2,3},{3,4},{4,5},{5,6},{6,7},{7,8},{8,9},{9,10},{10,1... | collective-permute-start | bytes 49160 | tf_op jit(solution)/shard_map/ppermute | solution.py:263
  45.2 7.7 %collective-permute-start.3 = (f32[32,128]{1,0:T(8,128)S(1)}, f32[32,128]{1,0:T(8,128)S(1)}, u32[]{:S(2)}, u32[]{:S(2)}) collective-permute-start(f32[32,128]{1,0:T(8,128)S(1)} %get-tuple-element.20), channel_id=1, source_target_pairs={{1,0},{2,1},{3,2},{4,3},{5,4},{6,5},{7,6},{8,7},{9,8},{10,9},{11,1... | collective-permute-start | bytes 49160 | tf_op jit(solution)/shard_map/ppermute | solution.py:264
